TPU v7x, 32 devices: a whole 2x2x4 slice. The times are simulated.
32 devices in a mesh: dp: 2 (over x), row: 4 (over z), col: 4 (over y, core).
Axes of the slice: x: 2, y: 2, z: 4, core: 2. Of those that a mesh axis runs over, the one named last changes fastest.
Arguments:
- tokens: bfloat16 [4, 8, 1024, 768], P(None, None, 'col', ('dp', 'row')), may hold values from -6 to 6
- cotangent: bfloat16 [4, 8, 1024, 768], P(None, ('dp', 'row'), 'col'), may hold values from -6 to 6
- lengths: int32 [4, 8], replicated, may hold values from 1 to 1024, 5120 in all within a row
- seq_order: int32 [4, 8], replicated, may hold values from 0 to 7, each once within a row
- w_qkv: bfloat16 [768, 2304], P(('dp', 'row'), 'col'), may hold values from -0.21875 to 0.21875
- w_out: bfloat16 [768, 768], P(('dp', 'row'), 'col'), may hold values from -2 to 2
- w_up: bfloat16 [768, 3072], P(('dp', 'row'), 'col'), may hold values from -0.21875 to 0.21875
- w_down: bfloat16 [3072, 768], P(('dp', 'row'), 'col'), may hold values from -0.109375 to 0.109375
- gain_one: bfloat16 [768], P(('dp', 'row', 'col')), may hold values from 0.5 to 1.5
- shift_one: bfloat16 [768], P(('dp', 'row', 'col')), may hold values from -1 to 1
- gain_two: bfloat16 [768], P(('dp', 'row', 'col')), may hold values from 0.5 to 1.5
- shift_two: bfloat16 [768], P(('dp', 'row', 'col')), may hold values from -1 to 1
Outputs:
- output: bfloat16 [4, 8, 1024, 768], P(None, ('dp', 'row'), 'col')
- tokens_grad: bfloat16 [4, 8, 1024, 768], P(None, None, 'col', ('dp', 'row'))
- w_qkv_grad: float32 [768, 2304], P(('dp', 'row'), 'col')
- w_out_grad: float32 [768, 768], P(('dp', 'row'), 'col')
- w_up_grad: float32 [768, 3072], P(('dp', 'row'), 'col')
- w_down_grad: float32 [3072, 768], P(('dp', 'row'), 'col')
- gain_one_grad: float32 [768], P(('dp', 'row', 'col'))
- shift_one_grad: float32 [768], P(('dp', 'row', 'col'))
- gain_two_grad: float32 [768], P(('dp', 'row', 'col'))
- shift_two_grad: float32 [768], P(('dp', 'row', 'col'))
Inputs may be any that keep to these rules, and one draw needn't show every extreme that they name: `seq_order`: each row is a permutation of the micro-batch's 8 sequences. In every micro-batch the lengths add up to 5120, and the longest is 1024.
All inputs are finite; a program needn't handle non-finite values.
Results may differ from a plain program's by a relative error of at most 0.017.
Values may be sent and summed in bfloat16 or wider, within the bound.
A program may use at most 256 MiB of HBM per device.

v0:
```python
import jax
import jax.numpy as jnp
from jax import lax
from jax.sharding import PartitionSpec as P

HEAD = 64


NEGATIVE = -1000000000.0
EPSILON = 1e-12
ROOT_HALF = 0.7071067811865476


def layer_norm(values, factor, offset):
    average = jnp.mean(values, axis=-1, keepdims=True)
    centered = values - average
    variance = jnp.mean(centered * centered, axis=-1, keepdims=True)
    return centered * lax.rsqrt(variance + EPSILON) * factor + offset


def gelu_act(values):
    return 0.5 * values * (1.0 + lax.erf(values * ROOT_HALF))


def product(left, right):
    return jnp.dot(left, right, preferred_element_type=jnp.float32)


def product_tn(left, right):
    return lax.dot_general(
        left, right, (((0,), (0,)), ((), ())), preferred_element_type=jnp.float32
    )


def product_nt(left, right):
    return lax.dot_general(
        left, right, (((1,), (1,)), ((), ())), preferred_element_type=jnp.float32
    )


def gather_layer(w_qkv, w_out, w_up, w_down, gain_one, shift_one, gain_two, shift_two):
    col_whole = (
        lax.all_gather(w_qkv, "col", axis=1, tiled=True),
        lax.all_gather(w_out, "col", axis=1, tiled=True),
        lax.all_gather(w_up, "col", axis=1, tiled=True),
        lax.all_gather(w_down, "col", axis=1, tiled=True),
        lax.all_gather(gain_one, "col", axis=0, tiled=True),
        lax.all_gather(shift_one, "col", axis=0, tiled=True),
        lax.all_gather(gain_two, "col", axis=0, tiled=True),
        lax.all_gather(shift_two, "col", axis=0, tiled=True),
    )
    return (
        lax.all_gather(col_whole[0], ("dp", "row"), axis=0, tiled=True),
        lax.all_gather(col_whole[1], ("dp", "row"), axis=0, tiled=True),
        lax.all_gather(col_whole[2], ("dp", "row"), axis=0, tiled=True),
        lax.all_gather(col_whole[3], ("dp", "row"), axis=0, tiled=True),
        lax.all_gather(col_whole[4], ("dp", "row"), axis=0, tiled=True),
        lax.all_gather(col_whole[5], ("dp", "row"), axis=0, tiled=True),
        lax.all_gather(col_whole[6], ("dp", "row"), axis=0, tiled=True),
        lax.all_gather(col_whole[7], ("dp", "row"), axis=0, tiled=True),
    )


def reduce_grads(grad_terms):
    row_part = (
        lax.psum_scatter(grad_terms[0], ("dp", "row"), scatter_dimension=0, tiled=True),
        lax.psum_scatter(grad_terms[1], ("dp", "row"), scatter_dimension=0, tiled=True),
        lax.psum_scatter(grad_terms[2], ("dp", "row"), scatter_dimension=0, tiled=True),
        lax.psum_scatter(grad_terms[3], ("dp", "row"), scatter_dimension=0, tiled=True),
        lax.psum_scatter(grad_terms[4], ("dp", "row"), scatter_dimension=0, tiled=True),
        lax.psum_scatter(grad_terms[5], ("dp", "row"), scatter_dimension=0, tiled=True),
        lax.psum_scatter(grad_terms[6], ("dp", "row"), scatter_dimension=0, tiled=True),
        lax.psum_scatter(grad_terms[7], ("dp", "row"), scatter_dimension=0, tiled=True),
    )
    return (
        lax.psum_scatter(
            row_part[0].astype(jnp.bfloat16), "col", scatter_dimension=1, tiled=True
        ).astype(jnp.float32),
        lax.psum_scatter(
            row_part[1].astype(jnp.bfloat16), "col", scatter_dimension=1, tiled=True
        ).astype(jnp.float32),
        lax.psum_scatter(
            row_part[2].astype(jnp.bfloat16), "col", scatter_dimension=1, tiled=True
        ).astype(jnp.float32),
        lax.psum_scatter(
            row_part[3].astype(jnp.bfloat16), "col", scatter_dimension=1, tiled=True
        ).astype(jnp.float32),
        lax.psum_scatter(
            row_part[4].astype(jnp.bfloat16), "col", scatter_dimension=0, tiled=True
        ).astype(jnp.float32),
        lax.psum_scatter(
            row_part[5].astype(jnp.bfloat16), "col", scatter_dimension=0, tiled=True
        ).astype(jnp.float32),
        lax.psum_scatter(
            row_part[6].astype(jnp.bfloat16), "col", scatter_dimension=0, tiled=True
        ).astype(jnp.float32),
        lax.psum_scatter(
            row_part[7].astype(jnp.bfloat16), "col", scatter_dimension=0, tiled=True
        ).astype(jnp.float32),
    )


def to_groups(slot_tokens):
    return lax.all_to_all(slot_tokens, ("dp", "row"), split_axis=1, concat_axis=3, tiled=True)


def from_groups(grouped_grad):
    return lax.all_to_all(grouped_grad, ("dp", "row"), split_axis=3, concat_axis=1, tiled=True)


def micro_step(rows_in, cot_rows, seq_lengths, layer_parts):
    w_qkv, w_out, w_up, w_down = (layer_parts[0], layer_parts[1], layer_parts[2], layer_parts[3])
    gain_one = layer_parts[4].astype(jnp.float32)
    shift_one = layer_parts[5].astype(jnp.float32)
    gain_two = layer_parts[6].astype(jnp.float32)
    shift_two = layer_parts[7].astype(jnp.float32)
    seq_group, quarter, model_width = rows_in.shape
    head_count = model_width // HEAD
    full_len = quarter * lax.axis_size("col")
    key_pos = jnp.arange(full_len, dtype=jnp.int32)
    flat_rows = rows_in.reshape(seq_group * quarter, model_width)
    qkv = (
        product(flat_rows, w_qkv).astype(jnp.bfloat16).reshape(seq_group, quarter, 3 * model_width)
    )
    queries = qkv[:, :, :model_width]
    key_vals = lax.all_gather(qkv[:, :, model_width:], "col", axis=1, tiled=True)

    def masked_scores(query_seq, kv_seq, seq_len):
        query_heads = query_seq.reshape(quarter, head_count, HEAD)
        key_heads = kv_seq[:, :model_width].reshape(full_len, head_count, HEAD)
        scores = (
            jnp.einsum("qhe,khe->hqk", query_heads, key_heads, preferred_element_type=jnp.float32)
            * 0.125
        )
        valid_keys = key_pos < seq_len
        return (jnp.where(valid_keys[None, None, :], scores, NEGATIVE), query_heads, key_heads)

    def attend(pieces):
        query_seq, kv_seq, seq_len = pieces
        scores, query_heads, key_heads = masked_scores(query_seq, kv_seq, seq_len)
        value_heads = kv_seq[:, model_width:].reshape(full_len, head_count, HEAD)
        row_top = jnp.max(scores, axis=-1, keepdims=True)
        exp_scores = jnp.exp(scores - row_top)
        row_total = jnp.sum(exp_scores, axis=-1, keepdims=True)
        attn_probs = (exp_scores / row_total).astype(jnp.bfloat16)
        log_total = row_top[:, :, 0] + jnp.log(row_total[:, :, 0])
        context = jnp.einsum(
            "hqk,khe->qhe", attn_probs, value_heads, preferred_element_type=jnp.float32
        )
        return (context.astype(jnp.bfloat16).reshape(quarter, model_width), log_total)

    context, log_totals = lax.map(attend, (queries, key_vals, seq_lengths))
    ctx_rows = context.reshape(seq_group * quarter, model_width)
    attn_out = product(ctx_rows, w_out)
    mixed = flat_rows.astype(jnp.float32) + attn_out
    hidden = layer_norm(mixed, gain_one, shift_one)
    hidden_low = hidden.astype(jnp.bfloat16)
    pre_act = product(hidden_low, w_up)
    act_low = gelu_act(pre_act).astype(jnp.bfloat16)
    summed = hidden + product(act_low, w_down)
    output = layer_norm(summed, gain_two, shift_two).astype(jnp.bfloat16)
    out_grad = cot_rows.reshape(seq_group * quarter, model_width).astype(jnp.float32)
    unused_two, norm_two_back = jax.vjp(layer_norm, summed, gain_two, shift_two)
    g_summed, g_gain_two, g_shift_two = norm_two_back(out_grad)
    d_down = g_summed.astype(jnp.bfloat16)
    g_down = product_tn(act_low, d_down)
    d_act = product_nt(d_down, w_down)
    unused_act, gelu_back = jax.vjp(gelu_act, pre_act)
    d_pre = gelu_back(d_act)[0].astype(jnp.bfloat16)
    g_up = product_tn(hidden_low, d_pre)
    g_hidden = g_summed + product_nt(d_pre, w_up)
    unused_one, norm_one_back = jax.vjp(layer_norm, mixed, gain_one, shift_one)
    g_mixed, g_gain_one, g_shift_one = norm_one_back(g_hidden)
    d_attn = g_mixed.astype(jnp.bfloat16)
    g_out = product_tn(ctx_rows, d_attn)
    d_context = (
        product_nt(d_attn, w_out).astype(jnp.bfloat16).reshape(seq_group, quarter, model_width)
    )

    def query_back(query_seq, kv_seq, seq_len, log_total, dctx_seq):
        scores, query_heads, key_heads = masked_scores(query_seq, kv_seq, seq_len)
        value_heads = kv_seq[:, model_width:].reshape(full_len, head_count, HEAD)
        dctx_heads = dctx_seq.reshape(quarter, head_count, HEAD)
        soft = jnp.exp(scores - log_total[:, :, None])
        d_probs = jnp.einsum(
            "qhe,khe->hqk", dctx_heads, value_heads, preferred_element_type=jnp.float32
        )
        row_delta = jnp.sum(soft * d_probs, axis=-1, keepdims=True)
        d_scores = (soft * (d_probs - row_delta)).astype(jnp.bfloat16)
        d_query = (
            jnp.einsum("hqk,khe->qhe", d_scores, key_heads, preferred_element_type=jnp.float32)
            * 0.125
        )
        return (soft, d_scores, row_delta, query_heads, dctx_heads, d_query)

    def attend_back(pieces):
        query_seq, kv_seq, seq_len, log_total, dctx_seq = pieces
        soft, d_scores, row_delta, query_heads, dctx_heads, d_query = query_back(
            query_seq, kv_seq, seq_len, log_total, dctx_seq
        )
        soft_low = soft.astype(jnp.bfloat16)
        d_key = (
            jnp.einsum("hqk,qhe->khe", d_scores, query_heads, preferred_element_type=jnp.float32)
            * 0.125
        )
        d_value = jnp.einsum(
            "hqk,qhe->khe", soft_low, dctx_heads, preferred_element_type=jnp.float32
        )
        kv_terms = jnp.concatenate(
            [d_key.reshape(full_len, model_width), d_value.reshape(full_len, model_width)], axis=-1
        )
        return (d_query.astype(jnp.bfloat16).reshape(quarter, model_width), kv_terms)

    d_queries, kv_terms = lax.map(
        attend_back, (queries, key_vals, seq_lengths, log_totals, d_context)
    )
    d_kv = lax.psum_scatter(kv_terms.astype(jnp.bfloat16), "col", scatter_dimension=1, tiled=True)
    d_qkv = jnp.concatenate([d_queries, d_kv], axis=-1).reshape(
        seq_group * quarter, 3 * model_width
    )
    g_qkv = product_tn(flat_rows, d_qkv)
    d_input = (g_mixed + product_nt(d_qkv, w_qkv)).astype(jnp.bfloat16)
    grad_terms = (g_qkv, g_out, g_up, g_down, g_gain_one, g_shift_one, g_gain_two, g_shift_two)
    return (
        output.reshape(seq_group, quarter, model_width),
        grad_terms,
        d_input.reshape(seq_group, quarter, model_width),
    )


def local(
    tokens,
    cotangent,
    lengths,
    seq_order,
    w_qkv,
    w_out,
    w_up,
    w_down,
    gain_one,
    shift_one,
    gain_two,
    shift_two,
):
    micro_count = tokens.shape[0]
    slot_tokens = jnp.take_along_axis(tokens, seq_order[:, :, None, None], axis=1)
    grouped = to_groups(slot_tokens)
    seq_group = grouped.shape[1]
    group_index = lax.axis_index(("dp", "row"))
    slot_ids = group_index * seq_group + jnp.arange(seq_group, dtype=jnp.int32)
    sources = jnp.take(seq_order, slot_ids, axis=1)
    seq_lengths = jnp.take_along_axis(lengths, sources, axis=1)
    outputs = []
    input_grads = []
    totals = None
    for micro_idx in range(micro_count):
        layer_parts = gather_layer(
            w_qkv, w_out, w_up, w_down, gain_one, shift_one, gain_two, shift_two
        )
        output, grad_terms, d_input = micro_step(
            grouped[micro_idx], cotangent[micro_idx], seq_lengths[micro_idx], layer_parts
        )
        outputs.append(output)
        input_grads.append(d_input)
        totals = grad_terms if totals is None else jax.tree.map(jnp.add, totals, grad_terms)
    totals = reduce_grads(totals)
    returned = from_groups(jnp.stack(input_grads, axis=0))
    inverse = jnp.argsort(seq_order, axis=1)
    tokens_grad = jnp.take_along_axis(returned, inverse[:, :, None, None], axis=1)
    return (
        jnp.stack(outputs, axis=0),
        tokens_grad,
        totals[0],
        totals[1],
        totals[2],
        totals[3],
        totals[4],
        totals[5],
        totals[6],
        totals[7],
    )


def solution(mesh):
    in_specs = (
        P(None, None, "col", ("dp", "row")),
        P(None, ("dp", "row"), "col", None),
        P(),
        P(),
        P(("dp", "row"), "col"),
        P(("dp", "row"), "col"),
        P(("dp", "row"), "col"),
        P(("dp", "row"), "col"),
        P(("dp", "row", "col")),
        P(("dp", "row", "col")),
        P(("dp", "row", "col")),
        P(("dp", "row", "col")),
    )
    out_specs = (
        P(None, ("dp", "row"), "col", None),
        P(None, None, "col", ("dp", "row")),
        P(("dp", "row"), "col"),
        P(("dp", "row"), "col"),
        P(("dp", "row"), "col"),
        P(("dp", "row"), "col"),
        P(("dp", "row", "col")),
        P(("dp", "row", "col")),
        P(("dp", "row", "col")),
        P(("dp", "row", "col")),
    )
    return jax.shard_map(local, mesh=mesh, in_specs=in_specs, out_specs=out_specs, check_vma=False)
```

profile of v0, /device:TPU:0, one launch (start us, length us, event | category | flops | bytes accessed | tf_op | source)
XLA Modules:
  0.0 1368.0 jit_solution(9399050156364436209)
XLA Ops:
  7.2 8.8 all-gather
  19.3 67.9 %all_to_all.33 = bf16[4,8,256,96]{2,3,0,1:T(8,128)(2,1)S(1)} all-to-all(bf16[4,8,256,96]{2,3,0,1:T(8,128)(2,1)S(1)} %copy.144), channel_id=1, replica_groups=mesh['dp'=2,'row'=4,'col'=4] {'dp','row'}, dimensions={1} | all-to-all | bytes 3145728 | tf_op jit(solution)/shard_map/all_to_all | solution.py:104
  87.5 18.2 %all-gather.10.cloned.1.call-done = bf16[768,2304]{1,0:T(8,128)(2,1)} async-done(((bf16[96,2304]{1,0:T(8,128)(2,1)}), bf16[768,2304]{1,0:T(8,128)(2,1)}) %all-gather.10.cloned.1.call-update) | async-done | bytes 3538960 | tf_op jit(solution)/shard_map/all_gather | solution.py:53
  110.1 5.7 all_gather.43
  116.6 3.3 fusion.31
  127.3 11.7 all_gather.49
  139.1 8.1 all_gather.51
  150.3 7.4 all-reduce.19
  158.5 19.6 %all-reduce.17 = (bf16[768]{0:T(1024)(128)(2,1)S(1)}, bf16[768]{0:T(1024)(128)(2,1)S(1)}, bf16[768]{0:T(1024)(128)(2,1)S(1)}, bf16[768]{0:T(1024)(128)(2,1)S(1)}) all-reduce(bf16[768]{0:T(1024)(128)(2,1)S(1)} %dynamic-update-slice.4, bf16[768]{0:T(1024)(128)(2,1)S(1)} %dynamic-update-slice.2, ...), channel_id=1, replica_groups=mesh['dp'=2,'row'=4,'col'=4] {'dp','row'}, use_global_device_ids=true, to_apply=%add.3 | all-reduce | flops 3072 | bytes 12288
  200.3 3.3 fusion.26
  208.4 3.9 fusion.53
  214.4 3.2 fusion.163
  221.0 22.0 %all-gather.12.cloned.1.call-done = bf16[1,1024,1536]{2,1,0:T(8,128)(2,1)} async-done(((bf16[1,256,1536]{2,1,0:T(8,128)(2,1)}), bf16[1,1024,1536]{2,1,0:T(8,128)(2,1)}) %all-gather.12.cloned.1.call-update) | async-done | bytes 3145744 | tf_op jit(solution)/shard_map/all_gather | solution.py:126
  243.0 3.8 fusion.160
  259.1 3.9 fusion.52
  264.5 60.4 %all-gather.16.cloned.1.call-done = bf16[768,3072]{1,0:T(8,128)(2,1)} async-done(((bf16[96,3072]{1,0:T(8,128)(2,1)}), bf16[768,3072]{1,0:T(8,128)(2,1)}) %all-gather.16.cloned.1.call-update) | async-done | bytes 4718608 | tf_op jit(solution)/shard_map/all_gather | solution.py:55
  324.9 6.1 multiply_convert_fusion.9
  330.9 75.1 %all-gather.18.cloned.1.call-done = bf16[3072,768]{0,1:T(8,128)(2,1)} async-done(((bf16[384,768]{0,1:T(8,128)(2,1)}), bf16[3072,768]{0,1:T(8,128)(2,1)}) %all-gather.18.cloned.1.call-update) | async-done | bytes 4718608 | tf_op jit(solution)/shard_map/all_gather | solution.py:56
  406.1 4.5 fusion.169
  417.7 3.9 fusion.55
  422.4 12.0 all-gather.20.cloned.1.call-done
  434.4 3.7 fusion.161
  443.4 3.4 fusion.25
  453.0 4.2 fusion.54
  473.6 3.9 add_convert_fusion
  481.8 3.5 add_convert_fusion.1
  486.8 3.5 add_convert_fusion.2
  491.9 3.7 add_convert_fusion.3
  495.6 3.7 multiply_reduce_fusion.7
  503.7 6.6 fusion.38
  510.3 9.6 multiply_reduce_fusion.1
  519.9 6.7 multiply_convert_fusion.1
  533.7 12.5 multiply_reduce_fusion.3
  548.2 7.1 multiply_convert_fusion.3
  567.0 12.0 multiply_reduce_fusion.2
  580.5 6.9 multiply_convert_fusion.2
  598.9 12.1 multiply_reduce_fusion
  611.5 6.7 multiply_convert_fusion
  636.7 5.1 fusion.127
  641.8 5.2 fusion.130
  647.0 12.6 add_add_fusion
  660.3 3.4 fusion.140
  663.8 5.3 fusion.148
  669.1 5.2 fusion.144
  674.3 12.5 add_add_fusion.1
  688.3 4.8 fusion.51
  693.1 5.0 fusion.50
  698.1 5.0 fusion.49
  705.2 5.2 fusion.84
  710.4 5.2 fusion.86
  715.6 5.2 fusion.85
  720.8 11.6 add_add_fusion.2
  732.5 30.9 %reduce-scatter.29.cloned.1.call-done = f32[96,768]{1,0:T(8,128)} async-done(((f32[768,768]{1,0:T(8,128)}), f32[96,768]{1,0:T(8,128)}) %reduce-scatter.29.cloned.1.call-update) | async-done | bytes 294928 | tf_op jit(solution)/shard_map/reduce_scatter | solution.py:67
  765.6 3.5 fusion.56
  772.5 156.9 %reduce-scatter.35.cloned.1.call-done = f32[384,768]{1,0:T(8,128)} async-done(((f32[3072,768]{1,0:T(8,128)}), f32[384,768]{1,0:T(8,128)}) %reduce-scatter.35.cloned.1.call-update) | async-done | bytes 1179664 | tf_op jit(solution)/shard_map/reduce_scatter | solution.py:69
  937.5 4.5 all-to-all-start.1
  942.9 187.7 %reduce-scatter.31.cloned.1.call-done = f32[96,3072]{1,0:T(8,128)} async-done(((f32[768,3072]{1,0:T(8,128)}), f32[96,3072]{1,0:T(8,128)}) %reduce-scatter.31.cloned.1.call-update) | async-done | bytes 1179664 | tf_op jit(solution)/shard_map/reduce_scatter | solution.py:68
  1134.6 37.8 %all-reduce.16 = (bf16[768]{0:T(1024)(128)(2,1)S(1)}, bf16[768]{0:T(1024)(128)(2,1)S(1)}, bf16[768]{0:T(1024)(128)(2,1)S(1)}, bf16[768]{0:T(1024)(128)(2,1)S(1)}) all-reduce(f32[768]{0:T(1024)S(1)} %add_add_fusion.15, f32[768]{0:T(1024)S(1)} %add_add_fusion.14, ...), channel_id=14, replica_groups=mesh['dp'=2,'row'=4,'col'=4] {'dp','row'}, use_global_device_ids=true, to_apply=%region_61.63.clone | all-reduce | flops 3072 | bytes 18432
  1172.7 6.0 all-reduce.18
  1178.7 84.4 %reduce-scatter.27.cloned.1.call-done = f32[96,2304]{1,0:T(8,128)} async-done(((f32[768,2304]{1,0:T(8,128)}), f32[96,2304]{1,0:T(8,128)}) %reduce-scatter.27.cloned.1.call-update) | async-done | bytes 884752 | tf_op jit(solution)/shard_map/reduce_scatter | solution.py:66
  1269.2 15.8 %reduce-scatter.39.cloned.1.call-done = bf16[192,96]{1,0:T(8,128)(2,1)} async-done(((bf16[768,96]{1,0:T(8,128)(2,1)}), bf16[192,96]{1,0:T(8,128)(2,1)}) %reduce-scatter.39.cloned.1.call-update) | async-done | bytes 36880
  1292.7 16.9 %reduce-scatter.41.cloned.1.call-done = bf16[192,384]{1,0:T(8,128)(2,1)} async-done(((bf16[768,384]{1,0:T(8,128)(2,1)}), bf16[192,384]{1,0:T(8,128)(2,1)}) %reduce-scatter.41.cloned.1.call-update) | async-done | bytes 147472
  1311.5 22.9 %reduce-scatter.33.cloned.1.call-done = bf16[96,768]{1,0:T(8,128)(2,1)} async-done(((bf16[96,3072]{1,0:T(8,128)(2,1)}), bf16[96,768]{1,0:T(8,128)(2,1)}) %reduce-scatter.33.cloned.1.call-update) | async-done | bytes 147472 | tf_op jit(solution)/shard_map/reduce_scatter | solution.py:82
  1336.0 23.0 %reduce-scatter.37.cloned.1.call-done = bf16[576,96]{1,0:T(8,128)(2,1)} async-done(((bf16[2304,96]{1,0:T(8,128)(2,1)}), bf16[576,96]{1,0:T(8,128)(2,1)}) %reduce-scatter.37.cloned.1.call-update) | async-done | bytes 110608
  (665 shorter events, 204.0 us)
Async XLA Ops:
  7.2 98.5 %all-gather.10.cloned.1.call-start = ((), (), s32[]{:S(2)}) async-start(), calls=%async_computation.14 | async-start | bytes 3981312 | tf_op jit(solution)/shard_map/all_gather | solution.py:53
  17.5 178.3 %all-gather.22.cloned.1.call-start = ((), (), s32[]{:S(2)}) async-start(), calls=%async_computation.20 | async-start | bytes 3932160 | tf_op jit(solution)/shard_map/all_gather | solution.py:126
  87.4 96.8 %copy-start.63 = (bf16[1,1,256,8,96]{2,4,3,1,0:T(8,128)(2,1)}, bf16[1,1,256,8,96]{2,4,3,1,0:T(8,128)(2,1)S(1)}, u32[]{:S(2)}) copy-start(bf16[1,1,256,8,96]{2,4,3,1,0:T(8,128)(2,1)S(1)} %get-tuple-element.346) | copy-start | bytes 1179652
  87.5 97.8 %copy-start.65 = (bf16[1,1,256,8,96]{2,4,3,1,0:T(8,128)(2,1)}, bf16[1,1,256,8,96]{2,4,3,1,0:T(8,128)(2,1)S(1)}, u32[]{:S(2)}) copy-start(bf16[1,1,256,8,96]{2,4,3,1,0:T(8,128)(2,1)S(1)} %get-tuple-element.345) | copy-start | bytes 1179652
  87.5 98.7 %copy-start.61 = (bf16[1,1,256,8,96]{2,4,3,1,0:T(8,128)(2,1)}, bf16[1,1,256,8,96]{2,4,3,1,0:T(8,128)(2,1)S(1)}, u32[]{:S(2)}) copy-start(bf16[1,1,256,8,96]{2,4,3,1,0:T(8,128)(2,1)S(1)} %get-tuple-element.344) | copy-start | bytes 1179652
  87.5 100.6 %copy-start.59 = (bf16[1,1,256,8,96]{2,4,3,1,0:T(8,128)(2,1)}, bf16[1,1,256,8,96]{2,4,3,1,0:T(8,128)(2,1)S(1)}, u32[]{:S(2)}) copy-start(bf16[1,1,256,8,96]{2,4,3,1,0:T(8,128)(2,1)S(1)} %get-tuple-element.347) | copy-start | bytes 1179652
  108.8 79.2 %copy-start.82 = (bf16[1,256,2304]{2,1,0:T(8,128)(2,1)}, bf16[1,256,2304]{2,1,0:T(8,128)(2,1)S(1)}, u32[]{:S(2)}) copy-start(bf16[1,256,2304]{2,1,0:T(8,128)(2,1)S(1)} %fusion.30) | copy-start | bytes 3538948
  109.9 102.5 %all-gather.14.cloned.1.call-start = ((), (), s32[]{:S(2)}) async-start(), calls=%async_computation.16 | async-start | bytes 1327104 | tf_op jit(solution)/shard_map/all_gather | solution.py:54
  116.6 97.8 %all-gather.24.cloned.1.call-start = ((), (), s32[]{:S(2)}) async-start(), calls=%async_computation.21 | async-start | bytes 3932160 | tf_op jit(solution)/shard_map/all_gather | solution.py:126
  121.9 121.1 %all-gather.12.cloned.1.call-start = ((), (), s32[]{:S(2)}) async-start(), calls=%async_computation.15 | async-start | bytes 3932160 | tf_op jit(solution)/shard_map/all_gather | solution.py:126
  126.2 52.6 %copy-start.6 = (s32[4,8]{1,0:T(4,128)S(1)}, s32[4,8]{1,0:T(4,128)}, u32[]{:S(2)}) copy-start(s32[4,8]{1,0:T(4,128)} %param.16) | copy-start | bytes 388
  127.2 197.7 %all-gather.16.cloned.1.call-start = ((), (), s32[]{:S(2)}) async-start(), calls=%async_computation.17 | async-start | bytes 5308416 | tf_op jit(solution)/shard_map/all_gather | solution.py:55
  139.0 267.1 %all-gather.18.cloned.1.call-start = ((), (), s32[]{:S(2)}) async-start(), calls=%async_computation.18 | async-start | bytes 5308416 | tf_op jit(solution)/shard_map/all_gather | solution.py:56
  147.2 287.2 %all-gather.20.cloned.1.call-start = ((), (), s32[]{:S(2)}) async-start(), calls=%async_computation.19 | async-start | bytes 3932160 | tf_op jit(solution)/shard_map/all_gather | solution.py:126
  147.3 43.9 %copy-start.127 = (s32[4,8]{0,1:T(8,128)}, s32[4,8]{0,1:T(8,128)S(1)}, u32[]{:S(2)}) copy-start(s32[4,8]{0,1:T(8,128)S(1)} %copy.149) | copy-start | bytes 388
  178.1 289.2 %copy-start.98 = (f32[768]{0:T(1024)}, f32[768]{0:T(1024)S(1)}, u32[]{:S(2)}) copy-start(f32[768]{0:T(1024)S(1)} %convert_element_type.362) | copy-start | bytes 9220
  193.4 58.9 %copy-start.52 = (bf16[1,256,768]{1,2,0:T(8,128)(2,1)}, bf16[1,256,768]{1,2,0:T(8,128)(2,1)S(1)}, u32[]{:S(2)}) copy-start(bf16[1,256,768]{1,2,0:T(8,128)(2,1)S(1)} %copy.164) | copy-start | bytes 1179652
  195.3 509.9 %reduce-scatter.23.cloned.1.call-start = ((), (), s32[]{:S(2)}) async-start(), calls=%async_computation.24 | async-start | bytes 3932160 | tf_op jit(solution)/shard_map/reduce_scatter | solution.py:217
  221.0 31.3 %copy-start.20 = (bf16[1024,768]{0,1:T(8,128)(2,1)}, bf16[1024,768]{0,1:T(8,128)(2,1)S(1)}, u32[]{:S(2)}) copy-start(bf16[1024,768]{0,1:T(8,128)(2,1)S(1)} %copy.165) | copy-start | bytes 4718596
  263.0 67.9 %copy-start.76 = (bf16[12,64,256]{2,1,0:T(8,128)(2,1)}, bf16[12,64,256]{2,1,0:T(8,128)(2,1)S(1)}, u32[]{:S(2)}) copy-start(bf16[12,64,256]{2,1,0:T(8,128)(2,1)S(1)} %fusion.52) | copy-start | bytes 1179652
  264.5 231.1 %copy-start.130 = (f32[256]{0:T(256)}, f32[256]{0:T(256)S(1)}, u32[]{:S(2)}) copy-start(f32[256]{0:T(256)S(1)} %get-tuple-element.417) | copy-start | bytes 3076
  264.5 234.9 %copy-start.121 = (f32[256]{0:T(256)}, f32[256]{0:T(256)S(1)}, u32[]{:S(2)}) copy-start(f32[256]{0:T(256)S(1)} %get-tuple-element.416) | copy-start | bytes 3076
  422.4 77.0 %copy-start.12 = (f32[256,768]{1,0:T(8,128)}, f32[256,768]{1,0:T(8,128)S(1)}, u32[]{:S(2)}) copy-start(f32[256,768]{1,0:T(8,128)S(1)} %get-tuple-element.383) | copy-start | bytes 2359300
  422.4 77.0 %copy-start.116 = (f32[256]{0:T(256)}, f32[256]{0:T(256)S(1)}, u32[]{:S(2)}) copy-start(f32[256]{0:T(256)S(1)} %broadcast_multiply_fusion.7) | copy-start | bytes 3076
  457.8 41.6 %copy-start.14 = (f32[256,768]{1,0:T(8,128)}, f32[256,768]{1,0:T(8,128)S(1)}, u32[]{:S(2)}) copy-start(f32[256,768]{1,0:T(8,128)S(1)} %get-tuple-element.391) | copy-start | bytes 2359300
  457.9 41.6 %copy-start.118 = (f32[256]{0:T(256)}, f32[256]{0:T(256)S(1)}, u32[]{:S(2)}) copy-start(f32[256]{0:T(256)S(1)} %broadcast_multiply_fusion.5) | copy-start | bytes 3076
  458.3 41.1 %copy-start.123 = (f32[256]{0:T(256)}, f32[256]{0:T(256)S(1)}, u32[]{:S(2)}) copy-start(f32[256]{0:T(256)S(1)} %get-tuple-element.415) | copy-start | bytes 3076
  458.3 41.1 %copy-start.125 = (f32[256]{0:T(256)}, f32[256]{0:T(256)S(1)}, u32[]{:S(2)}) copy-start(f32[256]{0:T(256)S(1)} %get-tuple-element.414) | copy-start | bytes 3076
  465.8 29.8 %copy-start.151 = (f32[256]{0:T(256)}, f32[256]{0:T(256)S(1)}, u32[]{:S(2)}) copy-start(f32[256]{0:T(256)S(1)} %fusion.101) | copy-start | bytes 3076
  531.2 179.2 %reduce-scatter.19.cloned.1.call-start = ((), (), s32[]{:S(2)}) async-start(), calls=%async_computation.22 | async-start | bytes 3932160 | tf_op jit(solution)/shard_map/reduce_scatter | solution.py:217
  563.2 152.4 %reduce-scatter.21.cloned.1.call-start = ((), (), s32[]{:S(2)}) async-start(), calls=%async_computation.23 | async-start | bytes 3932160 | tf_op jit(solution)/shard_map/reduce_scatter | solution.py:217
  595.1 125.7 %reduce-scatter.25.cloned.1.call-start = ((), (), s32[]{:S(2)}) async-start(), calls=%async_computation.25 | async-start | bytes 3932160 | tf_op jit(solution)/shard_map/reduce_scatter | solution.py:217
  626.4 137.1 %reduce-scatter.29.cloned.1.call-start = ((), (), s32[]{:S(2)}) async-start(), calls=%async_computation.27 | async-start | bytes 2654208 | tf_op jit(solution)/shard_map/reduce_scatter | solution.py:67
  632.5 296.8 %reduce-scatter.35.cloned.1.call-start = ((), (), s32[]{:S(2)}) async-start(), calls=%async_computation.30 | async-start | bytes 10616832 | tf_op jit(solution)/shard_map/reduce_scatter | solution.py:69
  659.7 470.9 %reduce-scatter.31.cloned.1.call-start = ((), (), s32[]{:S(2)}) async-start(), calls=%async_computation.28 | async-start | bytes 10616832 | tf_op jit(solution)/shard_map/reduce_scatter | solution.py:68
  686.9 576.3 %reduce-scatter.27.cloned.1.call-start = ((), (), s32[]{:S(2)}) async-start(), calls=%async_computation.26 | async-start | bytes 7962624 | tf_op jit(solution)/shard_map/reduce_scatter | solution.py:66
  732.4 33.1 %copy-start.42 = (f32[256,768]{1,0:T(8,128)S(1)}, f32[256,768]{1,0:T(8,128)}, u32[]{:S(2)}) copy-start(f32[256,768]{1,0:T(8,128)} %get-tuple-element.357) | copy-start | bytes 2359300
  732.4 33.1 %copy-start.155 = (f32[256]{0:T(256)S(1)}, f32[256]{0:T(256)}, u32[]{:S(2)}) copy-start(f32[256]{0:T(256)} %copy-done.153) | copy-start | bytes 3076
  732.5 552.5 %reduce-scatter.39.cloned.1.call-start = ((), (), s32[]{:S(2)}) async-start(), calls=%async_computation.32 | async-start | bytes 245760
  765.3 544.3 %reduce-scatter.41.cloned.1.call-start = ((), (), s32[]{:S(2)}) async-start(), calls=%async_computation.33 | async-start | bytes 737280
  772.5 159.3 %copy-start.35 = (f32[256,768]{1,0:T(8,128)S(1)}, f32[256,768]{1,0:T(8,128)}, u32[]{:S(2)}) copy-start(f32[256,768]{1,0:T(8,128)} %get-tuple-element.311) | copy-start | bytes 2359300
  772.5 159.3 %copy-start.101 = (bf16[1,256,1536]{1,2,0:T(8,128)(2,1)S(1)}, bf16[1,256,1536]{1,2,0:T(8,128)(2,1)}, u32[]{:S(2)}) copy-start(bf16[1,256,1536]{1,2,0:T(8,128)(2,1)} %reduce-scatter.19.cloned.1.call-done) | copy-start | bytes 2359300
  772.5 159.4 %copy-start.162 = (f32[256]{0:T(256)S(1)}, f32[256]{0:T(256)}, u32[]{:S(2)}) copy-start(f32[256]{0:T(256)} %copy-done.161) | copy-start | bytes 3076
  937.4 195.4 %copy-start.17 = (bf16[4,1,256,768]{3,2,1,0:T(8,128)(2,1)S(1)}, bf16[4,1,256,768]{3,2,1,0:T(8,128)(2,1)}, u32[]{:S(2)}) copy-start(bf16[4,1,256,768]{3,2,1,0:T(8,128)(2,1)} %param.15) | copy-start | bytes 4718596
  937.4 196.9 %copy-start.135 = (f32[768]{0:T(1024)S(1)}, f32[768]{0:T(1024)}, u32[]{:S(2)}) copy-start(f32[768]{0:T(1024)} %get-tuple-element.280) | copy-start | bytes 9220
  937.4 197.0 %copy-start.136 = (f32[768]{0:T(1024)S(1)}, f32[768]{0:T(1024)}, u32[]{:S(2)}) copy-start(f32[768]{0:T(1024)} %get-tuple-element.360) | copy-start | bytes 9220
  937.4 197.0 %copy-start.137 = (f32[768]{0:T(1024)S(1)}, f32[768]{0:T(1024)}, u32[]{:S(2)}) copy-start(f32[768]{0:T(1024)} %get-tuple-element.363) | copy-start | bytes 9220
  937.5 197.0 %copy-start.175 = (f32[768]{0:T(1024)S(1)}, f32[768]{0:T(1024)}, u32[]{:S(2)}) copy-start(f32[768]{0:T(1024)} %get-tuple-element.284) | copy-start | bytes 9220
  937.5 197.0 %copy-start.132 = (f32[768]{0:T(1024)S(1)}, f32[768]{0:T(1024)}, u32[]{:S(2)}) copy-start(f32[768]{0:T(1024)} %get-tuple-element.291) | copy-start | bytes 9220
  937.5 197.0 %copy-start.133 = (f32[768]{0:T(1024)S(1)}, f32[768]{0:T(1024)}, u32[]{:S(2)}) copy-start(f32[768]{0:T(1024)} %get-tuple-element.358) | copy-start | bytes 9220
  937.5 197.0 %copy-start.134 = (f32[768]{0:T(1024)S(1)}, f32[768]{0:T(1024)}, u32[]{:S(2)}) copy-start(f32[768]{0:T(1024)} %get-tuple-element.361) | copy-start | bytes 9220
  937.5 197.0 %copy-start.174 = (f32[768]{0:T(1024)S(1)}, f32[768]{0:T(1024)}, u32[]{:S(2)}) copy-start(f32[768]{0:T(1024)} %get-tuple-element.293) | copy-start | bytes 9220
  937.5 197.0 %copy-start.138 = (f32[768]{0:T(1024)S(1)}, f32[768]{0:T(1024)}, u32[]{:S(2)}) copy-start(f32[768]{0:T(1024)} %get-tuple-element.270) | copy-start | bytes 9220
  937.5 197.0 %copy-start.139 = (f32[768]{0:T(1024)S(1)}, f32[768]{0:T(1024)}, u32[]{:S(2)}) copy-start(f32[768]{0:T(1024)} %get-tuple-element.338) | copy-start | bytes 9220
  937.5 197.0 %copy-start.140 = (f32[768]{0:T(1024)S(1)}, f32[768]{0:T(1024)}, u32[]{:S(2)}) copy-start(f32[768]{0:T(1024)} %get-tuple-element.340) | copy-start | bytes 9220
  937.5 197.0 %copy-start.141 = (f32[768]{0:T(1024)S(1)}, f32[768]{0:T(1024)}, u32[]{:S(2)}) copy-start(f32[768]{0:T(1024)} %get-tuple-element.343) | copy-start | bytes 9220
  937.5 349.0 %all-to-all-start.1 = ((bf16[4,1,256,768]{2,0,1,3:T(4,128)(2,1)}), bf16[4,1,256,768]{2,0,1,3:T(4,128)(2,1)}, u32[]{:S(2)}, u32[]{:S(2)}) async-start(bf16[4,1,256,768]{2,0,1,3:T(4,128)(2,1)} %copy.172), calls=%async_computation.5 | async-start | bytes 3145728 | tf_op jit(solution)/shard_map/all_to_all | solution.py:108
  942.0 392.3 %reduce-scatter.33.cloned.1.call-start = ((), (), s32[]{:S(2)}) async-start(), calls=%async_computation.29 | async-start | bytes 737280 | tf_op jit(solution)/shard_map/reduce_scatter | solution.py:82
  942.8 325.0 %copy-start.94 = (bf16[1,1,256,768]{3,2,1,0:T(8,128)(2,1)S(1)}, bf16[1,1,256,768]{3,2,1,0:T(8,128)(2,1)}, u32[]{:S(2)}) copy-start(bf16[1,1,256,768]{3,2,1,0:T(8,128)(2,1)} %get-tuple-element.348) | copy-start | bytes 1179652
  942.8 325.0 %copy-start.95 = (bf16[1,1,256,768]{3,2,1,0:T(8,128)(2,1)S(1)}, bf16[1,1,256,768]{3,2,1,0:T(8,128)(2,1)}, u32[]{:S(2)}) copy-start(bf16[1,1,256,768]{3,2,1,0:T(8,128)(2,1)} %get-tuple-element.349) | copy-start | bytes 1179652
  942.8 325.0 %copy-start.96 = (bf16[1,1,256,768]{3,2,1,0:T(8,128)(2,1)S(1)}, bf16[1,1,256,768]{3,2,1,0:T(8,128)(2,1)}, u32[]{:S(2)}) copy-start(bf16[1,1,256,768]{3,2,1,0:T(8,128)(2,1)} %get-tuple-element.350) | copy-start | bytes 1179652
  942.9 325.0 %copy-start.97 = (bf16[1,1,256,768]{3,2,1,0:T(8,128)(2,1)S(1)}, bf16[1,1,256,768]{3,2,1,0:T(8,128)(2,1)}, u32[]{:S(2)}) copy-start(bf16[1,1,256,768]{3,2,1,0:T(8,128)(2,1)} %get-tuple-element.351) | copy-start | bytes 1179652
  1132.8 226.2 %reduce-scatter.37.cloned.1.call-start = ((), (), s32[]{:S(2)}) async-start(), calls=%async_computation.31 | async-start | bytes 737280
  1288.1 72.6 %copy-start.1 = (bf16[4,8,256,96]{2,3,1,0:T(8,128)(2,1)S(1)}, bf16[4,8,256,96]{2,3,1,0:T(8,128)(2,1)}, u32[]{:S(2)}) copy-start(bf16[4,8,256,96]{2,3,1,0:T(8,128)(2,1)} %param.14) | copy-start | bytes 4718596
  (161 other events, 896.9 us)
Sparse Core Ops, SparseCore 0:
  17.6 88.0 all-gather.9
  110.0 30.2 all-gather.21
  143.0 41.2 all-gather.13
  185.7 27.2 all-gather.23
  214.4 28.5 all-gather.11
  245.0 79.8 all-gather.15
  326.9 79.1 all-gather.17
  407.6 26.7 all-gather.19
  531.3 37.9 reduce-scatter.22
  571.8 37.9 reduce-scatter.18
  612.4 37.9 reduce-scatter.20
  652.9 37.9 reduce-scatter.24
  694.4 68.9 reduce-scatter.28
  766.9 162.4 reduce-scatter.34
  932.8 197.7 reduce-scatter.30
  1134.1 128.9 reduce-scatter.26
  1266.2 18.7 reduce-scatter.38
  1287.5 22.0 reduce-scatter.40
  1312.2 22.0 reduce-scatter.32
  1336.8 22.0 reduce-scatter.36
where the time goes:
time: 1380 us; the launch traced here: 1370 us
  waiting for transfers between devices  727 us (53%)
  matrix products  269 us (19%)
  blocking collectives  173 us (13%)
  local copies, waits for them, and re-layouts  91.9 us (7%)
  other arithmetic  81 us (6%)
  between operations  20.1 us (1%)
    reduce_scatter x1, waiting for transfers between devices, reduce_grads(): lax.psum_scatter(grad_terms[2], ('dp', 'row'), scatter_dimension=0, tiled...  188 us
    reduce_scatter x1, waiting for transfers between devices, reduce_grads(): lax.psum_scatter(grad_terms[3], ('dp', 'row'), scatter_dimension=0, tiled...  157 us
    reduce_scatter x1, waiting for transfers between devices, reduce_grads(): lax.psum_scatter(grad_terms[0], ('dp', 'row'), scatter_dimension=0, tiled...  84.4 us
    dot_general x16, matrix products, product_tn(): lax.dot_general(left, right, (((0,), (0,)), ((), ())), preferred_element_...  83.7 us
    all_gather x1, waiting for transfers between devices, gather_layer(): lax.all_gather(col_whole[3], ('dp', 'row'), axis=0, tiled=True)  75.1 us
    unnamed x4, blocking collectives  70.8 us
    all_to_all x1, blocking collectives, to_groups(): lax.all_to_all(slot_tokens, ('dp', 'row'), split_axis=1, concat_axis=3, t...  67.9 us
    all_gather x1, waiting for transfers between devices, gather_layer(): lax.all_gather(col_whole[2], ('dp', 'row'), axis=0, tiled=True)  60.4 us
  transfers between devices with their start and end apart: 21, of which 13 were waited for; matrix products, arithmetic and copies ran while one was open for 23% of the time, Pallas kernels for 0%

commit v1 on v0

v1 whole, which is shorter than its diff:
```python
import functools

import jax
import jax.numpy as jnp
from jax import lax
from jax.experimental import pallas as pl
from jax.experimental.pallas import tpu as pltpu
from jax.sharding import PartitionSpec as P

HEAD = 64
NEGATIVE = -1000000000.0
EPSILON = 1e-12
ROOT_HALF = 0.7071067811865476
MESH = pl.DeviceIdType.MESH
BF = jnp.bfloat16
F32 = jnp.float32


def aligned(value, step):
    return pl.multiple_of(value, step)


class Place:
    def __init__(self, n_dp, n_row, n_col):
        self.n_dp, self.n_row, self.n_col = n_dp, n_row, n_col
        self.n = n_dp * n_row * n_col
        self.x = lax.axis_index("dp")
        self.z = lax.axis_index("row")
        self.c = lax.axis_index("col")
        self.y, self.k = self.c // 2, self.c % 2
        self.g = self.x * n_row + self.z
        self.flat = self.g * n_col + self.c

    def of_flat(self, flat):
        group = flat // self.n_col
        return (group // self.n_row, group % self.n_row, flat % self.n_col)

    def dev(self, x=None, z=None, y=None, k=None):
        x = self.x if x is None else x
        z = self.z if z is None else z
        y = self.y if y is None else y
        k = self.k if k is None else k
        return (x, z, y * 2 + k)

    def barrier(self):
        sem = pltpu.get_barrier_semaphore()

        def greet(i, carry):
            pl.semaphore_signal(
                sem, inc=1, device_id=self.of_flat((self.flat + i) % self.n), device_id_type=MESH
            )
            return carry

        lax.fori_loop(1, self.n, greet, 0)
        pl.semaphore_wait(sem, self.n - 1)


class Lanes:
    def __init__(self, send_sems, recv_sems):
        self.send_sems, self.recv_sems, self.used, self.sent = send_sems, recv_sems, 0, []

    def slot(self):
        self.used += 1
        return self.used - 1

    def copy(self, src, dst, device, slot):
        return pltpu.make_async_remote_copy(
            src_ref=src, dst_ref=dst, send_sem=self.send_sems.at[slot],
            recv_sem=self.recv_sems.at[slot], device_id=device, device_id_type=MESH,
        )

    def send(self, src, dst, device):
        slot = self.slot()
        made = self.copy(src, dst, device, slot)
        made.start()
        self.sent.append(made)
        return slot

    def arrived(self, landing, slot, device):
        self.copy(landing, landing, device, slot).wait_recv()

    def finish(self):
        for made in self.sent:
            made.wait_send()
        self.sent = []


class Gather:
    def __init__(self, place, lanes, region, first):
        self.place, self.lanes, self.region, self.first = place, lanes, region, first
        self.slots = {}

    def start(self, own):
        p, lanes = self.place, self.lanes
        mine = self.region(p.x, p.z, 1, p.y, p.k, 1)
        for i in range(1, p.n_row):
            self.slots["z", i] = lanes.send(own, mine, p.dev(z=(p.z + i) % p.n_row))

    def hop(self):
        p, lanes = self.place, self.lanes
        for i in range(1, p.n_row):
            source = (p.z + p.n_row - i) % p.n_row
            lanes.arrived(self.region(p.x, source, 1, p.y, p.k, 1), self.slots["z", i], p.dev(z=source))
        line = self.region(p.x, 0, p.n_row, p.y, p.k, 1)
        if self.first == "x":
            self.slots["one"] = lanes.send(line, line, p.dev(x=1 - p.x))
            self.slots["two"] = lanes.send(line, line, p.dev(y=1 - p.y))
        else:
            self.slots["one"] = lanes.send(line, line, p.dev(y=1 - p.y))
            self.slots["two"] = lanes.send(line, line, p.dev(x=1 - p.x))
        self.slots["core"] = lanes.send(line, line, p.dev(k=1 - p.k))

    def turn(self):
        p, lanes = self.place, self.lanes
        if self.first == "x":
            peer, after = p.dev(x=1 - p.x), p.dev(y=1 - p.y)
            line = self.region(1 - p.x, 0, p.n_row, p.y, p.k, 1)
        else:
            peer, after = p.dev(y=1 - p.y), p.dev(x=1 - p.x)
            line = self.region(p.x, 0, p.n_row, 1 - p.y, p.k, 1)
        lanes.arrived(line, self.slots["one"], peer)
        self.slots["three"] = lanes.send(line, line, after)
        self.slots["core_one"] = lanes.send(line, line, p.dev(k=1 - p.k))

    def last(self):
        p, lanes = self.place, self.lanes
        if self.first == "x":
            peer = p.dev(y=1 - p.y)
            parts = (self.region(p.x, 0, p.n_row, 1 - p.y, p.k, 1), self.region(1 - p.x, 0, p.n_row, 1 - p.y, p.k, 1))
        else:
            peer = p.dev(x=1 - p.x)
            parts = (self.region(1 - p.x, 0, p.n_row, p.y, p.k, 1), self.region(1 - p.x, 0, p.n_row, 1 - p.y, p.k, 1))
        for name, part in zip(("two", "three"), parts):
            lanes.arrived(part, self.slots[name], peer)
            self.slots["core_" + name] = lanes.send(part, part, p.dev(k=1 - p.k))

    def end(self):
        p, lanes = self.place, self.lanes
        other, peer = 1 - p.k, p.dev(k=1 - p.k)
        lanes.arrived(self.region(p.x, 0, p.n_row, p.y, other, 1), self.slots["core"], peer)
        if self.first == "x":
            parts = ((1 - p.x, p.y), (p.x, 1 - p.y), (1 - p.x, 1 - p.y))
        else:
            parts = ((p.x, 1 - p.y), (1 - p.x, p.y), (1 - p.x, 1 - p.y))
        for name, (x, y) in zip(("core_one", "core_two", "core_three"), parts):
            lanes.arrived(self.region(x, 0, p.n_row, y, other, 1), self.slots[name], peer)


def rows_region(ref, n_row):
    width = ref.shape[3] // 2

    def region(x, z, nz, y, k, ny):
        if nz == 1:
            return ref.at[x * n_row + z, k, :, pl.ds(aligned(y * width, 128), width)]
        return ref.at[pl.ds(x * n_row + z, nz), k, :, pl.ds(aligned(y * width, 128), width)]

    return region


def lanes_region(ref, n_dp, n_row):
    width = ref.shape[3] // (n_dp * n_row)

    def region(x, z, nz, y, k, ny):
        return ref.at[y, k, :, pl.ds(aligned((x * n_row + z) * width, 128), nz * width)]

    return region


def gather_kernel(
    dims, seq_ref, tok_ref, cot_ref, qkv_ref, out_ref, up_ref, down_ref, norm_ref,
    xt_ref, cotf_ref, gqkv_ref, gout_ref, gup_ref, gdown_ref, gnorm_ref,
    tsend, half_qkv, half_out, half_up, pair_qkv, pair_out, pair_up,
    tok_send, tok_recv, cot_send, cot_recv, w_send, w_recv, local_sem,
):
    n_dp, n_row, n_col = dims
    p = Place(n_dp, n_row, n_col)
    micro, slots = tok_ref.shape[0], tok_ref.shape[1]
    span = tok_ref.shape[3]
    p.barrier()
    lanes = Lanes(w_send, w_recv)
    partner = p.dev(k=1 - p.k)
    halves = []
    for block, landing in ((qkv_ref, half_qkv), (out_ref, half_out), (up_ref, half_up)):
        rows = landing.shape[0]
        slot = lanes.send(block.at[pl.ds(aligned((1 - p.k) * rows, 16), rows), :], landing, partner)
        halves.append((block, landing, slot, rows))
    for m in range(micro):
        for j in range(slots):
            tsend[m * slots + j] = tok_ref[m, seq_ref[m, j]]

    def tok_copy(i):
        target = (p.flat + i) % p.n
        return pltpu.make_async_remote_copy(
            src_ref=tsend.at[(target % n_col) * slots + target // n_col],
            dst_ref=xt_ref.at[p.g, :, pl.ds(aligned(p.c * span, 128), span)],
            send_sem=tok_send.at[i], recv_sem=tok_recv.at[i],
            device_id=p.of_flat(target), device_id_type=MESH,
        )

    def tok_start(i, carry):
        tok_copy(i).start()
        return carry

    lax.fori_loop(1, p.n, tok_start, 0)
    own_tok = pltpu.make_async_copy(
        tsend.at[p.c * slots + p.g], xt_ref.at[p.g, :, pl.ds(aligned(p.c * span, 128), span)], local_sem.at[0]
    )
    own_tok.start()
    gathers = []
    locals_ = []
    specs = (
        (halves[0], pair_qkv, rows_region(gqkv_ref, n_row), "x"),
        (halves[1], pair_out, rows_region(gout_ref, n_row), "y"),
        (halves[2], pair_up, rows_region(gup_ref, n_row), "x"),
    )
    for index, ((block, landing, slot, rows), pair, region, first) in enumerate(specs):
        lanes.arrived(landing, slot, partner)
        mine = block[pl.ds(aligned(p.k * rows, 16), rows), :]
        theirs = landing[...]
        width = mine.shape[1]
        pair[:, :width] = jnp.where(p.k == 0, mine, theirs)
        pair[:, width:] = jnp.where(p.k == 0, theirs, mine)
        local = pltpu.make_async_copy(pair, region(p.x, p.z, 1, p.y, p.k, 1), local_sem.at[1 + index])
        local.start()
        locals_.append(local)
        gather = Gather(p, lanes, region, first)
        gather.start(pair)
        gathers.append(gather)
    for block, region, first in (
        (down_ref, lanes_region(gdown_ref, n_dp, n_row), "y"),
        (norm_ref, rows_region(gnorm_ref, n_row), "y"),
    ):
        local = pltpu.make_async_copy(block, region(p.x, p.z, 1, p.y, p.k, 1), local_sem.at[1 + len(gathers)])
        local.start()
        locals_.append(local)
        gather = Gather(p, lanes, region, first)
        gather.start(block)
        gathers.append(gather)

    rows = cot_ref.shape[1]

    def cot_copy(i):
        target = (p.c + i) % n_col
        return pltpu.make_async_remote_copy(
            src_ref=cot_ref.at[target], dst_ref=cotf_ref.at[p.c],
            send_sem=cot_send.at[i], recv_sem=cot_recv.at[i],
            device_id=(p.x, p.z, target), device_id_type=MESH,
        )

    for i in range(1, n_col):
        cot_copy(i).start()
    own_cot = pltpu.make_async_copy(cot_ref.at[p.c], cotf_ref.at[p.c], local_sem.at[6])
    own_cot.start()
    for local in locals_:
        local.wait()
    order = (gathers[0], gathers[3], gathers[2], gathers[1], gathers[4])
    for gather in order:
        gather.hop()
    for gather in order:
        gather.turn()
    for gather in order:
        gather.last()
    for gather in order:
        gather.end()
    own_tok.wait()
    own_cot.wait()

    def tok_wait(i, carry):
        source = (p.flat + p.n - i) % p.n
        landing = xt_ref.at[source // n_col, :, pl.ds(aligned((source % n_col) * span, 128), span)]
        pltpu.make_async_remote_copy(
            src_ref=landing, dst_ref=landing, send_sem=tok_send.at[i], recv_sem=tok_recv.at[i],
            device_id=p.of_flat(source), device_id_type=MESH,
        ).wait_recv()
        tok_copy(i).wait_send()
        return carry

    lax.fori_loop(1, p.n, tok_wait, 0)
    for i in range(1, n_col):
        source = (p.c + n_col - i) % n_col
        pltpu.make_async_remote_copy(
            src_ref=cotf_ref.at[source], dst_ref=cotf_ref.at[source],
            send_sem=cot_send.at[i], recv_sem=cot_recv.at[i],
            device_id=(p.x, p.z, source), device_id_type=MESH,
        ).wait_recv()
        cot_copy(i).wait_send()
    lanes.finish()


ANY = pl.BlockSpec(memory_space=pl.ANY)
VM = pl.BlockSpec(memory_space=pltpu.VMEM)
SM = pl.BlockSpec(memory_space=pltpu.SMEM)


def gather_all(dims, seq_order, tok_t, cot, w_qkv, w_out, w_up, w_down_t, norms):
    n_dp, n_row, n_col = dims
    groups = n_dp * n_row
    micro, slots, feats, span = tok_t.shape
    qr, qc = w_qkv.shape
    orow, oc = w_out.shape
    ur, uc = w_up.shape
    dr, dc = w_down_t.shape
    shape = jax.ShapeDtypeStruct
    outs = (
        shape((groups, feats, n_col * span), BF),
        shape((n_col,) + cot.shape[1:], BF),
        shape((groups, 2, qr // 2, qc * n_col), BF),
        shape((groups, 2, orow // 2, oc * n_col), BF),
        shape((groups, 2, ur // 2, uc * n_col), BF),
        shape((2, 2, dr, dc * groups), BF),
        shape((groups, 2, 16, 256), BF),
    )
    dma = pltpu.SemaphoreType.DMA
    return pl.pallas_call(
        functools.partial(gather_kernel, dims),
        out_shape=outs,
        in_specs=[SM, VM, ANY, VM, VM, VM, VM, VM],
        out_specs=[ANY] * 7,
        scratch_shapes=[
            pltpu.VMEM((micro * slots, feats, span), BF),
            pltpu.VMEM((qr // 2, qc), BF),
            pltpu.VMEM((orow // 2, oc), BF),
            pltpu.VMEM((ur // 2, uc), BF),
            pltpu.VMEM((qr // 2, qc * 2), BF),
            pltpu.VMEM((orow // 2, oc * 2), BF),
            pltpu.VMEM((ur // 2, uc * 2), BF),
            dma((n_dp * n_row * n_col,)), dma((n_dp * n_row * n_col,)),
            dma((n_col,)), dma((n_col,)),
            dma((80,)), dma((80,)), dma((8,)),
        ],
        compiler_params=pltpu.CompilerParams(
            collective_id=0, has_side_effects=True, vmem_limit_bytes=48 * 2**20
        ),
        name="gather_all",
    )(seq_order, tok_t, cot, w_qkv, w_out, w_up, w_down_t, norms)


class Reduce:
    def __init__(self, place, lanes, grad, b0, b1, b2, b3, kind, first):
        self.p, self.lanes, self.grad, self.b = place, lanes, grad, (b0, b1, b2, b3)
        self.kind, self.first, self.slots = kind, first, {}

    def start(self):
        p = self.p
        self.slots[0] = self.lanes.send(self.grad.at[:, 1 - p.k], self.b[0], p.dev(k=1 - p.k))

    def half(self, ref, axis, side):
        if self.kind == "rows" and axis == "x" or self.kind == "lanes" and axis == "y":
            if self.kind == "lanes":
                return ref.at[side]
            count = ref.shape[0] // 2
            return ref.at[pl.ds(side * count, count)]
        width = ref.shape[-1] // 2
        lead = (slice(None),) * (len(ref.shape) - 1)
        return ref.at[lead + (pl.ds(aligned(side * width, 128), width),)]

    def axes(self):
        return ("x", "y") if self.first == "x" else ("y", "x")

    def send_half(self, stage, axis):
        p = self.p
        side = p.x if axis == "x" else p.y
        peer = p.dev(x=1 - p.x) if axis == "x" else p.dev(y=1 - p.y)
        self.slots[stage] = self.lanes.send(self.half(self.b[stage - 1], axis, 1 - side), self.b[stage], peer)

    def add_half(self, stage, axis):
        p = self.p
        side = p.x if axis == "x" else p.y
        peer = p.dev(x=1 - p.x) if axis == "x" else p.dev(y=1 - p.y)
        self.lanes.arrived(self.b[stage], self.slots[stage], peer)
        add_into(self.b[stage], self.half(self.b[stage - 1], axis, side))

    def one(self):
        p = self.p
        self.lanes.arrived(self.b[0], self.slots[0], p.dev(k=1 - p.k))
        add_into(self.b[0], self.grad.at[:, p.k])
        self.send_half(1, self.axes()[0])

    def two(self):
        self.add_half(1, self.axes()[0])
        self.send_half(2, self.axes()[1])

    def part(self, z):
        ref = self.b[2]
        if self.kind == "rows":
            return ref.at[z]
        width = self.b[3].shape[-1]
        return ref.at[:, pl.ds(aligned(z * width, 128), width)]

    def three(self):
        p = self.p
        self.add_half(2, self.axes()[1])
        for i in range(1, p.n_row):
            target = (p.z + i) % p.n_row
            self.slots["z", i] = self.lanes.send(self.part(target), self.b[3].at[i - 1], p.dev(z=target))

    def four(self):
        p = self.p
        total = self.part(p.z)[...].astype(F32)
        for i in range(1, p.n_row):
            source = (p.z + p.n_row - i) % p.n_row
            self.lanes.arrived(self.b[3].at[i - 1], self.slots["z", i], p.dev(z=source))
            total = total + self.b[3][i - 1].astype(F32)
        return total


def add_into(target, term):
    shape = target.shape
    if len(shape) == 2:
        target[...] = (target[...].astype(F32) + term[...].astype(F32)).astype(BF)
        return

    def body(i, carry):
        target[i] = (target[i].astype(F32) + term[i].astype(F32)).astype(BF)
        return carry

    lax.fori_loop(0, shape[0], body, 0)


def reduce_kernel(
    dims, seq_ref, dxt_ref, outf_ref, gqkv_ref, gout_ref, gup_ref, gdown_ref,
    output_ref, tgrad_ref, rqkv_ref, rout_ref, rup_ref, rdown_ref,
    trecv, q0, q1, q2, q3, o0, o1, o2, o3, u0, u1, u2, u3, d0, d1, d2, d3,
    fq, fo, fu, tok_send, tok_recv, out_send, out_recv, w_send, w_recv, local_sem,
):
    n_dp, n_row, n_col = dims
    p = Place(n_dp, n_row, n_col)
    micro, slots = tgrad_ref.shape[0], tgrad_ref.shape[1]
    span = tgrad_ref.shape[3]
    p.barrier()
    lanes = Lanes(w_send, w_recv)
    partner = p.dev(k=1 - p.k)
    down = Reduce(p, lanes, gdown_ref, d0, d1, d2, d3, "lanes", "x")
    up = Reduce(p, lanes, gup_ref, u0, u1, u2, u3, "rows", "y")
    out = Reduce(p, lanes, gout_ref, o0, o1, o2, o3, "rows", "x")
    qkv = Reduce(p, lanes, gqkv_ref, q0, q1, q2, q3, "rows", "y")
    order = (down, up, out, qkv)
    for r in order:
        r.start()

    def tok_copy(i):
        target = (p.flat + i) % p.n
        return pltpu.make_async_remote_copy(
            src_ref=dxt_ref.at[target // n_col, :, pl.ds(aligned((target % n_col) * span, 128), span)],
            dst_ref=trecv.at[p.c * slots + p.g],
            send_sem=tok_send.at[i], recv_sem=tok_recv.at[i],
            device_id=p.of_flat(target), device_id_type=MESH,
        )

    def tok_start(i, carry):
        tok_copy(i).start()
        return carry

    lax.fori_loop(1, p.n, tok_start, 0)
    own_tok = pltpu.make_async_copy(
        dxt_ref.at[p.g, :, pl.ds(aligned(p.c * span, 128), span)], trecv.at[p.c * slots + p.g], local_sem.at[0]
    )
    own_tok.start()

    def out_copy(i):
        target = (p.c + i) % n_col
        return pltpu.make_async_remote_copy(
            src_ref=outf_ref.at[target], dst_ref=output_ref.at[p.c],
            send_sem=out_send.at[i], recv_sem=out_recv.at[i],
            device_id=(p.x, p.z, target), device_id_type=MESH,
        )

    for i in range(1, n_col):
        out_copy(i).start()
    own_out = pltpu.make_async_copy(outf_ref.at[p.c], output_ref.at[p.c], local_sem.at[1])
    own_out.start()
    for r in order:
        r.one()
    for r in order:
        r.two()
    for r in order:
        r.three()
    rdown_ref[...] = down.four()
    ends = []
    for r, temp, result in ((up, fu, rup_ref), (out, fo, rout_ref), (qkv, fq, rqkv_ref)):
        total = r.four()
        rows, width = total.shape[0], total.shape[1] // 2
        temp[...] = jnp.where(p.k == 0, total[:, width:], total[:, :width])
        where_ = result.at[pl.ds(aligned(p.k * rows, 16), rows), :]
        result[pl.ds(aligned(p.k * rows, 16), rows), :] = jnp.where(p.k == 0, total[:, :width], total[:, width:])
        slot = lanes.send(temp, where_, partner)
        ends.append((result, rows, slot))
    own_tok.wait()
    own_out.wait()

    def tok_wait(i, carry):
        source = (p.flat + p.n - i) % p.n
        landing = trecv.at[(source % n_col) * slots + source // n_col]
        pltpu.make_async_remote_copy(
            src_ref=landing, dst_ref=landing, send_sem=tok_send.at[i], recv_sem=tok_recv.at[i],
            device_id=p.of_flat(source), device_id_type=MESH,
        ).wait_recv()
        tok_copy(i).wait_send()
        return carry

    lax.fori_loop(1, p.n, tok_wait, 0)
    for m in range(micro):
        for s in range(slots):
            place = jnp.int32(0)
            for j in range(slots):
                place = jnp.where(seq_ref[m, j] == s, jnp.int32(j), place)
            tgrad_ref[m, s] = trecv[m * slots + place]
    for result, rows, slot in ends:
        lanes.arrived(result.at[pl.ds(aligned((1 - p.k) * rows, 16), rows), :], slot, partner)
    for i in range(1, n_col):
        source = (p.c + n_col - i) % n_col
        pltpu.make_async_remote_copy(
            src_ref=output_ref.at[source], dst_ref=output_ref.at[source],
            send_sem=out_send.at[i], recv_sem=out_recv.at[i],
            device_id=(p.x, p.z, source), device_id_type=MESH,
        ).wait_recv()
        out_copy(i).wait_send()
    lanes.finish()


def reduce_all(dims, seq_order, dxt, outf, g_qkv, g_out, g_up, g_down_t):
    n_dp, n_row, n_col = dims
    groups = n_dp * n_row
    micro, slots = seq_order.shape
    feats, span = dxt.shape[1], dxt.shape[2] // n_col
    shape = jax.ShapeDtypeStruct
    buffers = []
    for g in (g_qkv, g_out, g_up):
        r, _, h, c = g.shape
        buffers += [
            pltpu.VMEM((r, h, c), BF),
        ]
        if g is g_out:
            buffers += [pltpu.VMEM((r // 2, h, c), BF)]
        else:
            buffers += [pltpu.VMEM((r, h, c // 2), BF)]
        buffers += [pltpu.VMEM((r // 2, h, c // 2), BF), pltpu.VMEM((n_row - 1, h, c // 2), BF)]
    _, _, h, c = g_down_t.shape
    buffers += [
        pltpu.VMEM((2, h, c), BF), pltpu.VMEM((2, h, c // 2), BF), pltpu.VMEM((h, c // 2), BF),
        pltpu.VMEM((n_row - 1, h, c // groups), BF),
    ]
    outs = (
        shape((n_col,) + outf.shape[1:], BF),
        shape((micro, slots, feats, span), BF),
        shape((g_qkv.shape[2] * 2, g_qkv.shape[3] // n_col), F32),
        shape((g_out.shape[2] * 2, g_out.shape[3] // n_col), F32),
        shape((g_up.shape[2] * 2, g_up.shape[3] // n_col), F32),
        shape((h, c // groups), F32),
    )
    temps = [pltpu.VMEM((g.shape[2], g.shape[3] // n_col), F32) for g in (g_qkv, g_out, g_up)]
    dma = pltpu.SemaphoreType.DMA
    return pl.pallas_call(
        functools.partial(reduce_kernel, dims),
        out_shape=outs,
        in_specs=[SM, VM, ANY, VM, VM, VM, VM],
        out_specs=[ANY, VM, VM, VM, VM, VM],
        scratch_shapes=[pltpu.VMEM((micro * slots, feats, span), BF)] + buffers + temps + [
            dma((n_dp * n_row * n_col,)), dma((n_dp * n_row * n_col,)),
            dma((n_col,)), dma((n_col,)),
            dma((40,)), dma((40,)), dma((8,)),
        ],
        compiler_params=pltpu.CompilerParams(
            collective_id=1, has_side_effects=True, vmem_limit_bytes=56 * 2**20
        ),
        name="reduce_all",
    )(seq_order, dxt, outf, g_qkv, g_out, g_up, g_down_t)


def layer_norm(values, factor, offset):
    average = jnp.mean(values, axis=-1, keepdims=True)
    centered = values - average
    variance = jnp.mean(centered * centered, axis=-1, keepdims=True)
    return centered * lax.rsqrt(variance + EPSILON) * factor + offset


def gelu_act(values):
    return 0.5 * values * (1.0 + lax.erf(values * ROOT_HALF))


def product(left, right):
    return jnp.dot(left, right, preferred_element_type=F32)


def product_tn(left, right):
    return lax.dot_general(left, right, (((0,), (0,)), ((), ())), preferred_element_type=F32)


def product_nt(left, right):
    return lax.dot_general(left, right, (((1,), (1,)), ((), ())), preferred_element_type=F32)


def attention(qkv, length):
    rows, width = qkv.shape[0], qkv.shape[1] // 3
    heads = width // HEAD
    q, k, v = (qkv[:, i * width:(i + 1) * width].reshape(rows, heads, HEAD) for i in range(3))
    scores = jnp.einsum("qhe,khe->hqk", q, k, preferred_element_type=F32) * 0.125
    valid = jnp.arange(rows, dtype=jnp.int32) < length
    scores = jnp.where(valid[None, None, :], scores, NEGATIVE)
    top = jnp.max(scores, axis=-1, keepdims=True)
    exps = jnp.exp(scores - top)
    total = jnp.sum(exps, axis=-1, keepdims=True)
    probs = (exps / total).astype(BF)
    context = jnp.einsum("hqk,khe->qhe", probs, v, preferred_element_type=F32)
    return context.astype(BF).reshape(rows, width), top + jnp.log(total)


def attention_back(qkv, length, stats, d_context):
    rows, width = qkv.shape[0], qkv.shape[1] // 3
    heads = width // HEAD
    q, k, v = (qkv[:, i * width:(i + 1) * width].reshape(rows, heads, HEAD) for i in range(3))
    dc = d_context.reshape(rows, heads, HEAD)
    scores = jnp.einsum("qhe,khe->hqk", q, k, preferred_element_type=F32) * 0.125
    valid = jnp.arange(rows, dtype=jnp.int32) < length
    scores = jnp.where(valid[None, None, :], scores, NEGATIVE)
    soft = jnp.exp(scores - stats)
    d_probs = jnp.einsum("qhe,khe->hqk", dc, v, preferred_element_type=F32)
    delta = jnp.sum(soft * d_probs, axis=-1, keepdims=True)
    d_scores = (soft * (d_probs - delta)).astype(BF)
    dq = jnp.einsum("hqk,khe->qhe", d_scores, k, preferred_element_type=F32) * 0.125
    dk = jnp.einsum("hqk,qhe->khe", d_scores, q, preferred_element_type=F32) * 0.125
    dv = jnp.einsum("hqk,qhe->khe", soft.astype(BF), dc, preferred_element_type=F32)
    return jnp.concatenate([a.astype(BF).reshape(rows, width) for a in (dq, dk, dv)], axis=-1)


def middle(x, context, cot, w_out, w_up, w_down_t, gain_one, shift_one, gain_two, shift_two):
    mixed = x.astype(F32) + product(context, w_out)
    hidden = layer_norm(mixed, gain_one, shift_one)
    hidden_low = hidden.astype(BF)
    pre_act = product(hidden_low, w_up)
    act_low = gelu_act(pre_act).astype(BF)
    summed = hidden + product_nt(act_low, w_down_t)
    output = layer_norm(summed, gain_two, shift_two).astype(BF)
    _, norm_two_back = jax.vjp(layer_norm, summed, gain_two, shift_two)
    g_summed, g_gain_two, g_shift_two = norm_two_back(cot.astype(F32))
    d_down = g_summed.astype(BF)
    g_down_t = product_tn(d_down, act_low).astype(BF)
    d_act = product(d_down, w_down_t)
    _, gelu_back = jax.vjp(gelu_act, pre_act)
    d_pre = gelu_back(d_act)[0].astype(BF)
    g_up = product_tn(hidden_low, d_pre).astype(BF)
    g_hidden = g_summed + product_nt(d_pre, w_up)
    _, norm_one_back = jax.vjp(layer_norm, mixed, gain_one, shift_one)
    g_mixed, g_gain_one, g_shift_one = norm_one_back(g_hidden)
    d_attn = g_mixed.astype(BF)
    g_out = product_tn(context, d_attn).astype(BF)
    d_context = product_nt(d_attn, w_out).astype(BF)
    return output, g_mixed, d_context, g_down_t, g_up, g_out, (g_gain_one, g_shift_one, g_gain_two, g_shift_two)


def take_blocks(blocks, places):
    def body(place_ref, in_ref, out_ref):
        def step(i, carry):
            out_ref[i] = in_ref[place_ref[i]]
            return carry

        lax.fori_loop(0, blocks.shape[0], step, 0)

    return pl.pallas_call(
        body, out_shape=jax.ShapeDtypeStruct(blocks.shape, blocks.dtype), in_specs=[SM, VM], out_specs=VM,
        compiler_params=pltpu.CompilerParams(vmem_limit_bytes=48 * 2**20), name="take_blocks",
    )(places, blocks)


def own_length(lengths, seq_order):
    n_row = lax.axis_size("row")
    slot = lax.axis_index("dp") * n_row + lax.axis_index("row")
    micro = lax.axis_index("col")
    index = jnp.arange(seq_order.shape[1], dtype=jnp.int32)
    order = jnp.sum(jnp.where(jnp.arange(seq_order.shape[0])[:, None] == micro, seq_order, 0), axis=0)
    source = jnp.sum(jnp.where(index == slot, order, 0))
    mine = jnp.sum(jnp.where(jnp.arange(seq_order.shape[0])[:, None] == micro, lengths, 0), axis=0)
    return jnp.sum(jnp.where(index == source, mine, 0))


def local(
    tokens, cotangent, lengths, seq_order, w_qkv, w_out, w_up, w_down, gain_one, shift_one, gain_two, shift_two,
):
    dims = tuple(lax.axis_size(a) for a in ("dp", "row", "col"))
    n_dp, n_row, n_col = dims
    groups = n_dp * n_row
    micro, slots, span, feats = tokens.shape
    width = cotangent.shape[3]
    rows = span * n_col
    direct = n_dp == 2 and n_col == 4 and feats % 32 == 0 and w_qkv.shape[0] % 32 == 0
    tok_t = jnp.swapaxes(tokens, 2, 3)
    w_down_t = w_down.T
    norms = jnp.stack([gain_one, shift_one, gain_two, shift_two])
    length = own_length(lengths, seq_order)
    everyone = ("dp", "row", "col")
    if direct:
        packed = jnp.pad(norms, ((0, 12), (0, 128 - norms.shape[1])))
        xt, cot, f_qkv, f_out, f_up, f_down_t, f_norms = gather_all(
            dims, seq_order, tok_t, cotangent[:, 0], w_qkv, w_out, w_up, w_down_t, packed
        )
        xt = xt.reshape(width, rows)
        cot = cot.reshape(rows, width)
        f_qkv, f_out, f_up, f_down_t = (
            f_qkv.reshape(width, -1), f_out.reshape(width, -1), f_up.reshape(width, -1), f_down_t.reshape(width, -1)
        )
        f_norms = f_norms.reshape(groups, 2, 16, 2, 128)[:, :, :4, :, : norms.shape[1]]
        f_norms = f_norms.transpose(2, 0, 3, 1, 4).reshape(4, width)
    else:
        offset = jnp.arange(micro, dtype=jnp.int32)[:, None] * slots
        sent = take_blocks(tok_t.reshape(micro * slots, feats, span), (seq_order + offset).reshape(-1))
        sent = jnp.swapaxes(sent.reshape(micro, slots, feats, span), 0, 1).reshape(micro * slots, feats, span)
        got = lax.all_to_all(sent, everyone, split_axis=0, concat_axis=0, tiled=True)
        xt = got.reshape(groups, n_col, feats, span).transpose(0, 2, 1, 3).reshape(width, rows)
        cot = lax.all_to_all(cotangent[:, 0], "col", split_axis=0, concat_axis=0, tiled=True).reshape(rows, width)

        def whole(w, row_axes, col_axes):
            w = lax.all_gather(w, col_axes, axis=1, tiled=True)
            return lax.all_gather(w, row_axes, axis=0, tiled=True)

        f_qkv, f_out, f_up = (whole(w, ("dp", "row"), "col") for w in (w_qkv, w_out, w_up))
        f_down_t = whole(w_down_t, "col", ("dp", "row"))
        f_norms = lax.all_gather(norms, everyone, axis=1, tiled=True)
    gains = [f_norms[i].astype(F32) for i in range(4)]
    x = xt.T
    qkv = product(x, f_qkv).astype(BF)
    context, stats = attention(qkv, length)
    output, g_mixed, d_context, g_down_t, g_up, g_out, norm_grads = middle(
        x, context, cot, f_out, f_up, f_down_t, *gains
    )
    d_qkv = attention_back(qkv, length, stats, d_context)
    g_qkv = product(xt, d_qkv).astype(BF)
    dxt = (g_mixed + product_nt(d_qkv, f_qkv)).astype(BF).T
    n_sum = lax.psum_scatter(
        jnp.stack(norm_grads), everyone, scatter_dimension=1, tiled=True
    )
    if direct:
        output, tgrad, r_qkv, r_out, r_up, r_down_t = reduce_all(
            dims, seq_order, dxt.reshape(groups, feats, rows), output.reshape(n_col, span, width),
            g_qkv.reshape(groups, 2, -1, g_qkv.shape[1]), g_out.reshape(groups, 2, -1, g_out.shape[1]),
            g_up.reshape(groups, 2, -1, g_up.shape[1]), g_down_t.reshape(2, 2, -1, g_down_t.shape[1]),
        )
    else:
        output = lax.all_to_all(output.reshape(n_col, span, width), "col", split_axis=0, concat_axis=0, tiled=True)
        sent = dxt.reshape(groups, feats, n_col, span).transpose(0, 2, 1, 3).reshape(micro * slots, feats, span)
        got = lax.all_to_all(sent, everyone, split_axis=0, concat_axis=0, tiled=True)
        got = jnp.swapaxes(got.reshape(slots, micro, feats, span), 0, 1).reshape(micro * slots, feats, span)
        index = jnp.arange(slots, dtype=jnp.int32)
        inverse = jnp.sum(jnp.where(seq_order[:, :, None] == index, index[None, :, None], 0), axis=1)
        offset = jnp.arange(micro, dtype=jnp.int32)[:, None] * slots
        tgrad = take_blocks(got, (inverse + offset).reshape(-1)).reshape(micro, slots, feats, span)

        def parts(g, row_axes, col_axes):
            g = lax.psum_scatter(g, col_axes, scatter_dimension=1, tiled=True)
            return lax.psum_scatter(g, row_axes, scatter_dimension=0, tiled=True).astype(F32)

        r_qkv, r_out, r_up = (parts(g, ("dp", "row"), "col") for g in (g_qkv, g_out, g_up))
        r_down_t = parts(g_down_t, "col", ("dp", "row"))
    return (
        output[:, None], jnp.swapaxes(tgrad, 2, 3), r_qkv, r_out, r_up, r_down_t.T,
        n_sum[0], n_sum[1], n_sum[2], n_sum[3],
    )


def solution(mesh):
    rows = ("dp", "row")
    every = ("dp", "row", "col")
    in_specs = (
        P(None, None, "col", rows), P(None, rows, "col", None), P(), P(),
        P(rows, "col"), P(rows, "col"), P(rows, "col"), P(rows, "col"),
        P(every), P(every), P(every), P(every),
    )
    out_specs = (
        P(None, rows, "col", None), P(None, None, "col", rows),
        P(rows, "col"), P(rows, "col"), P(rows, "col"), P(rows, "col"),
        P(every), P(every), P(every), P(every),
    )
    return jax.shard_map(local, mesh=mesh, in_specs=in_specs, out_specs=out_specs, check_vma=False)
```

time: 1380 us -> 627 us (0.45)
  waiting for transfers between devices: 727 us -> 0 us
  Pallas kernels: 0 us -> 282 us
  blocking collectives: 173 us -> 42.2 us
  matrix products: 269 us -> 194 us
  local copies, waits for them, and re-layouts: 91.9 us -> 28.8 us
  between operations: 20.1 us -> 1.58 us
    reduce_scatter x9 -> x0, waiting for transfers between devices: 483 us -> none  [the longest x1 188 us: reduce_grads(): lax.psum_scatter(grad_terms[2], ('dp', 'row'), scatter_dimension=0, tiled...]
    pallas_call x0 -> x2, Pallas kernels: none -> 282 us  [the longest x1 145 us: reduce_all(): pl.pallas_call(functools.partial(reduce_kernel, dims), out_shape=outs, in...]
    all_gather x8 -> x0, waiting for transfers between devices: 188 us -> none  [the longest x1 75.1 us: gather_layer(): lax.all_gather(col_whole[3], ('dp', 'row'), axis=0, tiled=True)]
    all_to_all x1 -> x0, blocking collectives: 67.9 us -> none  [to_groups(): lax.all_to_all(slot_tokens, ('dp', 'row'), split_axis=1, concat_axis=3, t...]
    dot_general x16 -> x3, matrix products: 83.7 us -> 16.1 us  [product_tn(): lax.dot_general(left, right, (((0,), (0,)), ((), ())), preferred_element_...]
    unnamed x23 -> x0, waiting for transfers between devices: 56 us -> none
    all_gather x4 -> x0, blocking collectives: 34.3 us -> none  [the longest x1 11.7 us: gather_layer(): lax.all_gather(w_up, 'col', axis=1, tiled=True)]
    unnamed x4 -> x1, blocking collectives: 70.8 us -> 42.2 us
  transfers between devices with their start and end apart: 21 -> 0, of which waited for: 13 -> 0; matrix products, arithmetic and copies ran while one was open for 23% -> 0% of each run, Pallas kernels for 0% -> 0%
where the time goes in v1:
time: 627 us; the launch traced here: 618 us
  Pallas kernels  282 us (45%)
  matrix products  194 us (31%)
  other arithmetic  69.6 us (11%)
  blocking collectives  42.2 us (7%)
  local copies, waits for them, and re-layouts  28.8 us (5%)
    pallas_call x1, Pallas kernels, reduce_all(): pl.pallas_call(functools.partial(reduce_kernel, dims), out_shape=outs, in...  145 us
    pallas_call x1, Pallas kernels, gather_all(): pl.pallas_call(functools.partial(gather_kernel, dims), out_shape=outs, in...  137 us
    unnamed x1, blocking collectives  42.2 us
    convert_element_type x1, other arithmetic, attention_back(): d_scores = (soft * (d_probs - delta)).astype(BF)  40.8 us
    dot_general x5, matrix products, product(): return jnp.dot(left, right, preferred_element_type=F32)  39.2 us
    dot_general x1, matrix products, attention_back(): d_probs = jnp.einsum('qhe,khe->hqk', dc, v, preferred_element_type=F32)  32.1 us
    dot_general x4, matrix products, product_nt(): lax.dot_general(left, right, (((1,), (1,)), ((), ())), preferred_element_...  22.2 us
    dot_general x1, matrix products, attention(): jnp.einsum('qhe,khe->hqk', q, k, preferred_element_type=F32) * 0.125  20.1 us

profile of v1, /device:TPU:0, one launch (start us, length us, event | category | flops | bytes accessed | tf_op | source)
XLA Modules:
  0.0 618.3 jit_solution(10221254859122694590)
XLA Ops:
  0.7 0.8 select_reduce_fusion.1
  1.5 0.6 fusion.27
  2.1 1.3 fusion.28
  3.4 0.6 iota_compare_fusion.2
  4.0 0.7 fusion.21.norm_ref
  4.7 0.9 copy-done
  5.7 0.9 copy-done.1
  6.6 0.9 copy-done.2
  7.5 0.8 copy-done.3
  8.3 0.7 copy-done.4
  8.9 136.8 %gather_all.1 = (bf16[8,96,1024]{2,1,0:T(8,128)(2,1)S(1)}, bf16[4,256,768]{2,1,0:T(8,128)(2,1)S(1)}, bf16[8,2,48,2304]{3,2,1,0:T(8,128)(2,1)}, bf16[8,2,48,768]{...) custom-call(s32[4,8]{1,0:T(4,128)S(1)} %copy-done.4, ...), custom_call_target="tpu_custom_call" | custom-call | tf_op jit(solution)/shard_map/gather_all/pallas_call | solution.py:314
  145.7 1.0 copy-done.7
  146.8 0.3 convert_reduce_fusion
  147.1 0.7 reshape.234
  147.9 0.1 reshape.239
  148.0 0.1 reshape.237
  148.1 0.1 reshape.238
  148.2 0.1 reshape.236
  148.2 2.1 copy.49
  150.4 6.1 convolution_convert_fusion
  156.5 2.0 fusion.36
  158.5 1.6 copy.52
  160.1 1.7 copy.51
  161.8 3.1 copy.50
  165.0 20.1 %fusion.37 = (f32[12,1024]{1,0:T(8,128)S(1)}, f32[12,1024,1024]{1,2,0:T(8,128)}) fusion(bf16[1024,12,64]{0,2,1:T(8,128)(2,1)S(1)} %bitcast.93, bf16[1024,12,64]{0,2,1:T(8,128)(2,1)} %bitcast.95, pred[1024]{0:T(1024)(128)(4,1)S(1)} %iota_compare_fusion.2), kind=kOutput, calls=%fused_computation.94 | convolution fusion | flops 1648349184 | bytes 53527552 | tf_op jit(solution)/shard_map/qhe,khe->hqk/dot_general | solution.py:597
  185.1 19.2 %fusion = f32[12,1024]{1,0:T(8,128)S(1)} fusion(f32[12,1024,1024]{1,2,0:T(8,128)} %get-tuple-element.90, f32[12,1024]{1,0:T(8,128)S(1)} %get-tuple-element.89), kind=kLoop, calls=%fused_computation.6 | loop fusion | flops 25153536 | bytes 50429952 | tf_op jit(solution)/shard_map/reduce_sum | solution.py:602
  204.4 18.6 %fusion.12 = bf16[12,64,1024]{2,1,0:T(8,128)(2,1)S(1)} fusion(bf16[1024,12,64]{0,2,1:T(8,128)(2,1)S(1)} %bitcast.101, f32[12,1024,1024]{1,2,0:T(8,128)} %get-tuple-element.90, f32[12,1024]{1,0:T(8,128)S(1)} %fusion, f32[12,1024]{1,0:T(8,128)S(1)} %get-tuple-element.89), kind=kOutput, calls=%fused_computation.41 | convolution fusion | flops 1649147904 | bytes 53575680 | tf_op jit(solution)/shard_map/hqk,khe->qhe/dot_general | solution.py:604
  223.0 1.5 fusion.38
  224.5 0.4 multiply_reduce_fusion.6
  224.9 0.2 slice-done
  225.2 0.1 slice-done.1
  225.3 9.6 %multiply_convert_fusion.1 = (bf16[1024,3072]{1,0:T(8,128)(2,1)S(1)}, f32[1024,3072]{1,0:T(8,128)}) fusion(bf16[768,3072]{1,0:T(8,128)(2,1)S(1)} %bitcast.125, f32[1024,768]{0,1:T(8,128)S(1)} %get-tuple-element.92, f32[768]{0:T(1024)S(1)} %reshape.238, f32[768]{0:T(1024)S(1)} %reshape.237, f32[1024]{0:T(1024)S(1)} %fusion.25, ...), kind=kOutput, calls=%fused_computation.12 | convolution fusion | flops 4851499008 | bytes 26753024 | tf_op jit(solution)/shard_map/dot_general | solution.py:582
  234.9 5.2 fusion.39
  240.1 0.4 multiply_reduce_fusion.5
  240.5 1.5 copy-done.9
  242.0 1.0 multiply_reduce_fusion.1
  243.1 2.5 fusion.35
  245.6 13.7 %add_convert_fusion = bf16[1024,3072]{1,0:T(8,128)(2,1)} fusion(f32[1024,3072]{1,0:T(8,128)} %get-tuple-element.94, bf16[768,3072]{1,0:T(8,128)(2,1)S(1)} %bitcast.130, f32[1024,768]{0,1:T(8,128)S(1)} %get-tuple-element.76, f32[1024]{0:T(1024)S(1)} %negate_multiply_fusion.1), kind=kOutput, calls=%fused_computation.11 | convolution fusion | flops 4874305536 | bytes 26742784 | tf_op jit(solution)/shard_map/dot_general | solution.py:582
  259.3 6.7 %convolution_convert_fusion.1 = bf16[768,3072]{1,0:T(8,128)(2,1)} fusion(bf16[1024,3072]{1,0:T(8,128)(2,1)S(1)} %get-tuple-element.93, f32[1024,768]{0,1:T(8,128)S(1)} %get-tuple-element.76, f32[1024]{0:T(1024)S(1)} %negate_multiply_fusion.1), kind=kOutput, calls=%fused_computation.15 | convolution fusion | flops 4835770368 | bytes 14159872 | tf_op jit(solution)/shard_map/dot_general | solution.py:586
  266.0 8.8 %multiply_reduce_fusion.2 = (f32[768]{0:T(1024)S(1)}, f32[1024]{0:T(1024)S(1)}, f32[768]{0:T(1024)S(1)}, f32[1024,768]{0,1:T(8,128)S(1)}) fusion(f32[1024,768]{0,1:T(8,128)S(1)} %get-tuple-element.92, f32[1024]{0:T(1024)S(1)} %fusion.25, f32[1024]{0:T(1024)S(1)} %broadcast_multiply_fusion.1, f32[768]{0:T(1024)S(1)} %reshape.237, ...), kind=kOutput, calls=%fused_computation.23 | convolution fusion | flops 4839699456 | bytes 20472832 | tf_op jit(solution)/shard_map/dot_general | solution.py:590
  274.8 6.9 %convolution_convert_fusion.2 = bf16[768,3072]{1,0:T(8,128)(2,1)} fusion(bf16[1024,3072]{1,0:T(8,128)(2,1)S(1)} %copy-done.25, f32[1024,768]{0,1:T(8,128)S(1)} %get-tuple-element.92, f32[768]{0:T(1024)S(1)} %reshape.238, f32[768]{0:T(1024)S(1)} %reshape.237, f32[1024]{0:T(1024)S(1)} %fusion.25, f32[1024]{0:T(1024)S(1)} %broadcast_multiply_fusion.1), kind=kOutput, calls=%fused_computation.16 | convolution fusion | flops 4838129664 | bytes 14170112 | tf_op jit(solution)/shard_map/dot_general | solution.py:586
  281.7 0.8 fusion.34
  282.5 0.0 copy-start.23
  282.6 2.5 convolution_convert_fusion.5
  285.1 42.2 %all-reduce.1 = f32[4,768]{1,0:T(4,128)S(1)} all-reduce(f32[4,768]{1,0:T(4,128)S(1)} %pad_maximum_fusion.5), channel_id=2, replica_groups=mesh['dp'=2,'row'=4,'col'=4] {'dp','row','col'}, use_global_device_ids=true, to_apply=%region_19.20.clone | all-reduce | flops 3072 | bytes 24576
  327.3 0.1 constant_dynamic-slice_fusion
  327.4 0.5 slice_bitcast_fusion
  327.9 3.3 convolution_convert_fusion.4
  331.2 19.0 %fusion.9 = bf16[12,64,1024]{2,1,0:T(8,128)(2,1)} fusion(bf16[1024,12,64]{0,2,1:T(8,128)(2,1)S(1)} %bitcast.97, f32[12,1024,1024]{1,2,0:T(8,128)} %get-tuple-element.90, f32[12,1024]{1,0:T(8,128)S(1)} %log_add_fusion), kind=kOutput, calls=%fused_computation.39 | convolution fusion | flops 1636564992 | bytes 53526528 | tf_op jit(solution)/shard_map/hqk,qhe->khe/dot_general | solution.py:622
  350.1 2.6 copy.57
  352.7 32.1 %multiply_reduce_fusion = (f32[12,1024]{1,0:T(8,128)S(1)}, f32[12,1024,1024]{1,2,0:T(8,128)}) fusion(f32[12,1024,1024]{1,2,0:T(8,128)} %get-tuple-element.90, f32[12,1024]{1,0:T(8,128)S(1)} %log_add_fusion, bf16[1024,12,64]{0,2,1:T(8,128)(2,1)S(1)} %bitcast.98, bf16[1024,12,64]{0,2,1:T(8,128)(2,1)} %bitcast.100), kind=kOutput, calls=%fused_computation.1 | convolution fusion | flops 1648349184 | bytes 103907328 | tf_op jit(solution)/shard_map/qhe,khe->hqk/dot_general | solution.py:617
  384.8 40.8 %multiply_convert_fusion = bf16[12,1024,1024]{1,2,0:T(8,128)(2,1)} fusion(f32[12,1024,1024]{1,2,0:T(8,128)} %get-tuple-element.99, f32[12,1024,1024]{1,2,0:T(8,128)} %get-tuple-element.90, f32[12,1024]{1,0:T(8,128)S(1)} %get-tuple-element.98, f32[12,1024]{1,0:T(8,128)S(1)} %log_add_fusion), kind=kLoop, calls=%fused_computation | loop fusion | flops 50331648 | bytes 125927424 | tf_op jit(solution)/shard_map/convert_element_type | solution.py:619
  425.6 14.0 %multiply_convert_fusion.2 = bf16[12,64,1024]{2,1,0:T(8,128)(2,1)} fusion(bf16[1024,12,64]{0,2,1:T(8,128)(2,1)S(1)} %bitcast.94, bf16[12,1024,1024]{1,2,0:T(8,128)(2,1)} %multiply_convert_fusion), kind=kOutput, calls=%fused_computation.26 | convolution fusion | flops 1612185600 | bytes 28311552 | tf_op jit(solution)/shard_map/hqk,qhe->khe/dot_general | solution.py:621
  439.6 0.0 copy-start.16
  439.7 12.8 %multiply_convert_fusion.3 = bf16[12,64,1024]{2,1,0:T(8,128)(2,1)S(1)} fusion(bf16[1024,12,64]{0,2,1:T(8,128)(2,1)S(1)} %bitcast.96, bf16[12,1024,1024]{1,2,0:T(8,128)(2,1)} %multiply_convert_fusion), kind=kOutput, calls=%fused_computation.27 | convolution fusion | flops 1612185600 | bytes 28311552 | tf_op jit(solution)/shard_map/hqk,khe->qhe/dot_general | solution.py:620
  452.5 4.9 add_convert_fusion.2
  457.4 8.3 %convolution_convert_fusion.3 = bf16[768,2304]{1,0:T(8,128)(2,1)} fusion(bf16[768,1024]{1,0:T(8,128)(2,1)S(1)} %bitcast.90, bf16[1024,768]{0,1:T(8,128)(2,1)S(1)} %bitcast.108, bf16[1024,768]{0,1:T(8,128)(2,1)S(1)} %bitcast.106, bf16[1024,768]{0,1:T(8,128)(2,1)S(1)} %bitcast.111), kind=kOutput, calls=%fused_computation.17 | convolution fusion | flops 3639803904 | bytes 9830400 | tf_op jit(solution)/shard_map/dot_general | solution.py:582
  465.7 145.4 %reduce_all.1 = (bf16[4,256,768]{2,1,0:T(8,128)(2,1)}, bf16[4,8,96,256]{3,2,1,0:T(8,128)(2,1)}, f32[96,576]{1,0:T(8,128)}, f32[96,192]{1,0:T(8,128)}, f32[96,768]{1,0:T(8,128)}, /*index=5*/f32[192,384]{1,0:T(8,128)}) custom-call(s32[4,8]{1,0:T(4,128)} %seq_ref.3, bf16[8,96,1024]{2,1,0:T(8,128)(2,1)} %bitcast.109, bf16[4,256,768]{2,1,0:T(8,128)(2,1)} %bitcast.99, ...), custom_call_target="tpu_custom_call" | custom-call | tf_op jit(solution)/shard_map/reduce_all/pallas_call | solution.py:553
  611.1 2.8 copy.75
  613.9 1.1 copy.76
  615.1 0.7 copy.77
  615.8 0.6 copy.78
  616.4 0.7 copy.79
  617.1 0.7 copy.80
  (69 shorter events, 0.3 us)
Async XLA Ops:
  4.7 0.9 copy-start
  5.7 0.9 copy-start.1
  6.6 0.9 copy-start.2
  7.5 0.8 copy-start.3
  8.3 0.7 copy-start.4
  145.7 1.0 copy-start.7
  146.7 76.2 %copy-start.5 = (bf16[8,96,1024]{2,1,0:T(8,128)(2,1)}, bf16[8,96,1024]{2,1,0:T(8,128)(2,1)S(1)}, u32[]{:S(2)}) copy-start(bf16[8,96,1024]{2,1,0:T(8,128)(2,1)S(1)} %get-tuple-element.25) | copy-start | bytes 4718596
  161.8 23.3 %copy-start.10 = (bf16[1024,768]{0,1:T(8,128)(2,1)}, bf16[1024,768]{0,1:T(8,128)(2,1)S(1)}, u32[]{:S(2)}) copy-start(bf16[1024,768]{0,1:T(8,128)(2,1)S(1)} %copy.51) | copy-start | bytes 4718596
  185.1 19.2 %copy-start.13 = (bf16[1024,768]{0,1:T(8,128)(2,1)S(1)}, bf16[1024,768]{0,1:T(8,128)(2,1)}, u32[]{:S(2)}) copy-start(bf16[1024,768]{0,1:T(8,128)(2,1)} %copy.50) | copy-start | bytes 4718596
  204.3 18.6 %copy-start.8 = (bf16[8,2,48,768]{3,2,1,0:T(8,128)(2,1)S(1)}, bf16[8,2,48,768]{3,2,1,0:T(8,128)(2,1)}, u32[]{:S(2)}) copy-start(bf16[8,2,48,768]{3,2,1,0:T(8,128)(2,1)} %copy-done.7) | copy-start | bytes 3538948
  223.0 2.2 slice-start
  223.0 2.3 slice-start.1
  223.0 11.9 %slice-start.2 = ((s8[4718592]{0:T(1024)(128)(4,1)}), s8[4194304]{0:T(1024)(128)(4,1)S(1)}, s32[]{:S(2)}) async-start(s8[4718592]{0:T(1024)(128)(4,1)} %bitcast.127), calls=%async_computation.2 | async-start | bytes 8388608
  225.3 9.6 %slice-start.3 = ((s8[4718592]{0:T(1024)(128)(4,1)}), s8[524288]{0:T(1024)(128)(4,1)S(1)}, s32[]{:S(2)}) async-start(s8[4718592]{0:T(1024)(128)(4,1)} %bitcast.127), calls=%async_computation.3 | async-start | bytes 1048576
  240.1 1.9 copy-start.9
  266.0 8.9 %copy-start.25 = (bf16[1024,3072]{1,0:T(8,128)(2,1)S(1)}, bf16[1024,3072]{1,0:T(8,128)(2,1)}, u32[]{:S(2)}) copy-start(bf16[1024,3072]{1,0:T(8,128)(2,1)} %add_convert_fusion) | copy-start | bytes 18874372
  282.5 2.5 copy-start.14
  282.5 2.5 copy-start.23
  384.8 40.8 %copy-start.11 = (bf16[1024,768]{0,1:T(8,128)(2,1)S(1)}, bf16[1024,768]{0,1:T(8,128)(2,1)}, u32[]{:S(2)}) copy-start(bf16[1024,768]{0,1:T(8,128)(2,1)} %copy-done.10) | copy-start | bytes 4718596
  425.6 14.0 %copy-start.12 = (bf16[1024,768]{0,1:T(8,128)(2,1)S(1)}, bf16[1024,768]{0,1:T(8,128)(2,1)}, u32[]{:S(2)}) copy-start(bf16[1024,768]{0,1:T(8,128)(2,1)} %copy.52) | copy-start | bytes 4718596
  439.6 12.8 %copy-start.15 = (f32[1024,768]{0,1:T(8,128)S(1)}, f32[1024,768]{0,1:T(8,128)}, u32[]{:S(2)}) copy-start(f32[1024,768]{0,1:T(8,128)} %copy-done.14) | copy-start | bytes 9437188
  439.6 12.8 %copy-start.16 = (bf16[12,64,1024]{2,1,0:T(8,128)(2,1)S(1)}, bf16[12,64,1024]{2,1,0:T(8,128)(2,1)}, u32[]{:S(2)}) copy-start(bf16[12,64,1024]{2,1,0:T(8,128)(2,1)} %multiply_convert_fusion.2) | copy-start | bytes 4718596
  439.7 12.8 %copy-start.17 = (bf16[12,64,1024]{2,1,0:T(8,128)(2,1)S(1)}, bf16[12,64,1024]{2,1,0:T(8,128)(2,1)}, u32[]{:S(2)}) copy-start(bf16[12,64,1024]{2,1,0:T(8,128)(2,1)} %fusion.9) | copy-start | bytes 4718596
  439.7 12.8 %copy-start.24 = (bf16[8,2,48,2304]{3,2,1,0:T(8,128)(2,1)S(1)}, bf16[8,2,48,2304]{3,2,1,0:T(8,128)(2,1)}, u32[]{:S(2)}) copy-start(bf16[8,2,48,2304]{3,2,1,0:T(8,128)(2,1)} %get-tuple-element.26) | copy-start | bytes 10616836
  452.5 4.9 copy-start.6
  611.1 2.9 copy-start.18
  611.1 4.0 copy-start.21
  611.1 4.7 copy-start.22
  611.1 5.3 copy-start.20
  611.1 6.0 copy-start.19
